TPU v7x, 256 devices: a whole 4x4x8 slice. The times are simulated.
256 devices in a mesh: lat: 64 (over x_lo, z, y), lon: 4 (over x_hi, core).
Axes of the slice: x: 4 (x_hi: 2, x_lo: 2; x = x_hi * 2 + x_lo), y: 4, z: 8, core: 2. Of those that a mesh axis runs over, the one named last changes fastest.
Arguments:
- grid_field: bfloat16 [512, 1024, 256], P('lat', 'lon'), may hold values from -6 to 6
- basis_index: int32 [512, 25], P('lat'), may hold values from 0 to 4
- quad_weight: bfloat16 [512, 25], P('lat'), may hold values from 0.19921875 to 1
- disco_weight: bfloat16 [4, 2, 128, 128], replicated, may hold values from -0.25 to 0.25
- mode_order: int32 [512], replicated, may hold values from 0 to 511, each once
- legendre: bfloat16 [512, 512, 512], P(('lat', 'lon')), may hold values from -0.25 to 0.25
- filter_weight: bfloat16 [2, 256, 256], replicated, may hold values from -0.25 to 0.25
- inner_weight: bfloat16 [256, 512], replicated, may hold values from -0.375 to 0.375
- outer_weight: bfloat16 [512, 256], replicated, may hold values from -0.25 to 0.25
Outputs:
- layer_out: bfloat16 [512, 1024, 256], P('lat', 'lon')
Inputs may be any that keep to these rules, and one draw needn't show every extreme that they name: `basis_index`: A value below 4 names the basis function of a support point; the value 4 marks a point outside the filter's support. `mode_order`: every wavenumber 0 to 511 is held by exactly one slot.
All inputs are finite; a program needn't handle non-finite values.
Results may differ from a plain program's by a relative error of at most 0.017.
Values may be sent and summed in bfloat16 or wider, within the bound.
A program may use at most 128 MiB of HBM per device.

v0:
```python
import math

import jax
import jax.numpy as jnp
from jax import lax
from jax.sharding import PartitionSpec as P


def extended(cells, sides, width):
    for axis, dim in sides:
        count = lax.axis_size(axis)
        head = lax.slice_in_dim(cells, 0, width, axis=dim)
        tail = lax.slice_in_dim(cells, cells.shape[dim] - width, cells.shape[dim], axis=dim)
        cells = jnp.concatenate(
            [
                lax.ppermute(tail, axis, [(i, (i + 1) % count) for i in range(count)]),
                cells,
                lax.ppermute(head, axis, [((i + 1) % count, i) for i in range(count)]),
            ],
            axis=dim,
        )
    return cells


def twiddle(mode_ids, places, full_len, doubled):
    residue = (mode_ids[:, None] * places[None, :] % full_len).astype(jnp.float32)
    phase = residue * (2.0 * math.pi / full_len)
    factor = jnp.ones(mode_ids.shape, jnp.float32)
    if doubled:
        factor = jnp.where(mode_ids == 0, 1.0, 2.0).astype(jnp.float32)
    factor = factor[:, None] / math.sqrt(full_len)
    return jnp.stack([jnp.cos(phase) * factor, -jnp.sin(phase) * factor]).astype(jnp.bfloat16)


def spectral_matrix(filter_weight):
    real_part = filter_weight[0]
    imag_part = filter_weight[1]
    upper_half = jnp.concatenate([real_part, imag_part], axis=1)
    lower_half = jnp.concatenate([-imag_part, real_part], axis=1)
    return jnp.concatenate([upper_half, lower_half], axis=0)


def disco_layer(padded, basis_index, quad_weight, disco_weight, lat_rows, lon_cols):
    basis_count = disco_weight.shape[0]
    groups = disco_weight.shape[1]
    group_ch = disco_weight.shape[2]
    channels = groups * group_ch
    selector = jnp.where(
        basis_index[:, :, None] == jnp.arange(basis_count, dtype=jnp.int32)[None, None, :],
        quad_weight[:, :, None],
        jnp.zeros((), quad_weight.dtype),
    ).astype(jnp.float32)
    running = jnp.zeros((basis_count, lat_rows, lon_cols, channels), jnp.float32)
    for lat_off in range(5):
        for lon_off in range(5):
            point = 5 * lat_off + lon_off
            window = padded[lat_off : lat_off + lat_rows, lon_off : lon_off + lon_cols].astype(
                jnp.float32
            )
            scales = jnp.transpose(selector[:, point, :])
            running = running + scales[:, :, None, None] * window[None]
    response = running.astype(jnp.bfloat16).reshape(
        basis_count, lat_rows, lon_cols, groups, group_ch
    )
    mixed = jnp.einsum(
        "kajgi,kgio->ajgo", response, disco_weight, preferred_element_type=jnp.float32
    )
    return mixed.reshape(lat_rows, lon_cols, channels).astype(jnp.bfloat16)


def shards(
    grid_field,
    basis_index,
    quad_weight,
    disco_weight,
    mode_order,
    legendre,
    filter_weight,
    inner_weight,
    outer_weight,
):
    lat_rows, lon_cols, channels = grid_field.shape
    lat_count = lax.axis_size("lat")
    lon_count = lax.axis_size("lon")
    lat_pos = lax.axis_index("lat")
    lon_pos = lax.axis_index("lon")
    padded = extended(grid_field, (("lat", 0), ("lon", 1)), 2)
    rim_rows = jnp.arange(lat_rows + 4, dtype=jnp.int32)
    at_pole = (rim_rows < 2) & (lat_pos == 0) | (rim_rows >= lat_rows + 2) & (
        lat_pos == lat_count - 1
    )
    padded = jnp.where(at_pole[:, None, None], jnp.zeros((), padded.dtype), padded)
    disco_out = disco_layer(padded, basis_index, quad_weight, disco_weight, lat_rows, lon_cols)
    mode_count = mode_order.shape[0]
    total_lon = lon_cols * lon_count
    per_lon = mode_count // lon_count
    per_dev = per_lon // lat_count
    lon_share = channels // lon_count
    all_lons = jnp.arange(total_lon, dtype=jnp.int32)
    full_lon = lax.all_to_all(disco_out, "lon", split_axis=2, concat_axis=1, tiled=True)
    forward_tab = twiddle(mode_order, all_lons, total_lon, False)
    spectra = jnp.einsum(
        "rsl,alc->sarc", forward_tab, full_lon, preferred_element_type=jnp.float32
    ).astype(jnp.bfloat16)
    spectra = spectra.reshape(lat_count, lon_count, per_dev, lat_rows, 2, lon_share)
    arrived = lax.all_to_all(
        lax.all_to_all(spectra, "lat", split_axis=0, concat_axis=3, tiled=True),
        "lon",
        split_axis=1,
        concat_axis=5,
        tiled=True,
    )
    arrived = arrived.reshape(per_dev, lat_rows * lat_count, 2, channels)
    first_slot = (lat_pos * lon_count + lon_pos) * per_dev
    my_modes = lax.dynamic_slice_in_dim(mode_order, first_slot, per_dev)
    degrees = legendre.shape[1]
    allowed = jnp.arange(degrees, dtype=jnp.int32)[None, :] >= my_modes[:, None]
    legend_tab = jnp.where(allowed[:, :, None], legendre, jnp.zeros((), legendre.dtype))
    coeffs = jnp.einsum(
        "tla,tarc->tlrc", legend_tab, arrived, preferred_element_type=jnp.float32
    ).astype(jnp.bfloat16)
    filtered = (
        jnp.dot(
            coeffs.reshape(per_dev * degrees, 2 * channels),
            spectral_matrix(filter_weight),
            preferred_element_type=jnp.float32,
        )
        .astype(jnp.bfloat16)
        .reshape(per_dev, degrees, 2, channels)
    )
    back_spectra = jnp.einsum(
        "tla,tlrc->tarc", legend_tab, filtered, preferred_element_type=jnp.float32
    ).astype(jnp.bfloat16)
    sectioned = back_spectra.reshape(1, 1, per_dev, lat_rows * lat_count, 2, channels)
    returned = lax.all_to_all(
        lax.all_to_all(sectioned, "lat", split_axis=3, concat_axis=0, tiled=True),
        "lon",
        split_axis=5,
        concat_axis=1,
        tiled=True,
    )
    returned = returned.reshape(mode_count, lat_rows, 2, lon_share)
    inverse_tab = twiddle(mode_order, all_lons, total_lon, True)
    lon_waves = jnp.einsum(
        "rsl,sarc->alc", inverse_tab, returned, preferred_element_type=jnp.float32
    ).astype(jnp.bfloat16)
    spatial = lax.all_to_all(lon_waves, "lon", split_axis=1, concat_axis=2, tiled=True)
    mixed_in = jax.nn.gelu(
        spatial.astype(jnp.float32) + disco_out.astype(jnp.float32), approximate=True
    ).astype(jnp.bfloat16)
    hidden = jax.nn.gelu(
        jnp.dot(mixed_in.reshape(-1, channels), inner_weight, preferred_element_type=jnp.float32),
        approximate=True,
    ).astype(jnp.bfloat16)
    result = grid_field.astype(jnp.float32).reshape(-1, channels) + jnp.dot(
        hidden, outer_weight, preferred_element_type=jnp.float32
    )
    return result.reshape(lat_rows, lon_cols, channels).astype(jnp.bfloat16)


def solution(mesh):
    in_specs = (
        P("lat", "lon", None),
        P("lat", None),
        P("lat", None),
        P(),
        P(),
        P(("lat", "lon"), None, None),
        P(),
        P(),
        P(),
    )
    out_specs = P("lat", "lon", None)
    return jax.shard_map(shards, mesh=mesh, in_specs=in_specs, out_specs=out_specs, check_vma=False)
```

profile of v0, /device:TPU:1, one launch (start us, length us, event | category | flops | bytes accessed | tf_op | source)
XLA Modules:
  0.0 332.8 jit_solution(16614581098151910765)
XLA Ops:
  0.0 1.9 fusion.82
  1.9 2.1 collective-permute-start
  4.0 7.7 %collective-permute-start.1 = (bf16[2,256,256]{2,1,0:T(8,128)(2,1)}, bf16[2,256,256]{2,1,0:T(8,128)(2,1)S(1)}, u32[]{:S(2)}, u32[]{:S(2)}) collective-permute-start(bf16[2,256,256]{2,1,0:T(8,128)(2,1)} %get-tuple-element.32), channel_id=1, source_target_pairs={{4,0},{8,4},{12,8},{16,12},{20,16},{24,20},{28,24},{32,28},{36,32}... | collective-permute-start | bytes 786440 | tf_op jit(solution)/shard_map/ppermute | solution.py:18
  13.9 3.8 %collective-permute-done = bf16[2,256,256]{2,1,0:T(8,128)(2,1)S(1)} collective-permute-done((bf16[2,256,256]{2,1,0:T(8,128)(2,1)S(1)}, bf16[2,256,256]{2,1,0:T(8,128)(2,1)S(1)}, u32[]{:S(2)}, u32[]{:S(2)}) %collective-permute-start) | collective-permute-done | bytes 262176 | tf_op jit(solution)/shard_map/ppermute | solution.py:16
  17.9 3.6 %collective-permute-start.2 = (bf16[12,2,256]{2,1,0:T(2,128)(2,1)S(1)}, bf16[12,2,256]{2,1,0:T(2,128)(2,1)S(1)}, u32[]{:S(2)}, u32[]{:S(2)}) collective-permute-start(bf16[12,2,256]{2,1,0:T(2,128)(2,1)S(1)} %get-tuple-element.30), channel_id=1, source_target_pairs={{0,1},{1,2},{2,3},{3,0},{4,5},{5,6},{6,7},{7,4},{8,9},{9,10},{10,1... | collective-permute-start | bytes 36872 | tf_op jit(solution)/shard_map/ppermute | solution.py:16
  30.3 13.1 %convert_bitcast_fusion.24 = (f32[8,32,2,8,128]{4,3,2,1,0:T(8,128)}, f32[8,32,2,8,128]{4,3,2,1,0:T(8,128)}, f32[8,32,2,8,128]{4,3,2,1,0:T(8,128)}, f32[8,32,2,8,...) fusion(bf16[12,260,256]{2,1,0:T(8,128)(2,1)S(1)} %maximum_selec, ...), kind=kLoop, calls=%fused_computation.89 | loop fusion | flops 9961472 | bytes 59768832
  50.2 2.7 copy_bitcast_fusion.14
  53.9 2.7 copy_bitcast_fusion.12
  57.7 2.7 copy_bitcast_fusion.10
  61.4 2.7 copy_bitcast_fusion.8
  65.2 2.7 copy_bitcast_fusion.6
  68.9 2.7 copy_bitcast_fusion.4
  72.6 2.7 copy_bitcast_fusion.2
  76.4 2.6 copy_bitcast_fusion
  78.9 2.5 copy_bitcast_fusion.18
  81.4 2.5 copy_bitcast_fusion.20
  84.0 2.7 copy_bitcast_fusion.22
  87.7 24.3 %fusion.39 = bf16[8,256,2,128]{1,3,0,2:T(8,128)(2,1)S(1)} fusion(f32[8,256,2,128]{3,1,0,2:T(8,128)} %get-tuple-element.65, f32[4,8]{0,1:T(8,128)S(1)} %copy.321, f32[8,256,2,128]{3,1,0,2:T(8,128)} %get-tuple-element.66, f32[4,8]{0,1:T(8,128)S(1)} %copy.319, f32[8,256,2,128]{3,1,0,2:T(8,128)} %get-tuple-element.67, f32[4,8]{0,1:T(8,128)S(1)} %copy.317, ...), kind=kOutput, calls=%fused_computation.106 | convolution fusion | flops 642252800 | bytes 53742720 | tf_op jit(solution)/shard_map/kajgi,kgio->ajgo/dot_general | solution.py:65
  113.7 4.9 %all-to-all-start = ((bf16[8,256,256]{1,0,2:T(8,128)(2,1)}), bf16[8,256,256]{1,0,2:T(8,128)(2,1)S(1)}, u32[]{:S(2)}, u32[]{:S(2)}) async-start(bf16[8,256,256]{1,0,2:T(8,128)(2,1)} %copy.325), calls=%async_computation | async-start | bytes 2097152 | tf_op jit(solution)/shard_map/all_to_all | solution.py:100
  118.6 11.3 %multiply_convert_fusion.1 = (bf16[1,512,1024]{2,1,0:T(8,128)(2,1)}, bf16[1,512,1024]{2,1,0:T(8,128)(2,1)}, bf16[1,512,1024]{2,1,0:T(8,128)(2,1)}, bf16[1,512,1024]{2,1,0:T(8,128)(2,1)}) fusion(f32[512]{0:T(512)S(1)} %select_multiply_fusion, s32[512]{0:T(512)S(1)} %copy-done.32), kind=kLoop, calls=%fused_computation.91 | loop fusion | flops 12058624 | bytes 4198400 | tf_op jit(solution)/shard_map/convert.31
  129.9 3.8 %all-to-all-done = bf16[8,256,256]{1,0,2:T(8,128)(2,1)S(1)} async-done(((bf16[8,256,256]{1,0,2:T(8,128)(2,1)}), bf16[8,256,256]{1,0,2:T(8,128)(2,1)S(1)}, u32[]{:S(2)}, u32[]{:S(2)}) %all-to-all-start) | async-done | bytes 1048608 | tf_op jit(solution)/shard_map/all_to_all | solution.py:100
  136.1 3.8 %fusion.35 = bf16[512,8,2,64]{0,3,2,1:T(8,128)(2,1)} fusion(bf16[1,512,1024]{2,1,0:T(8,128)(2,1)} %get-tuple-element.64, bf16[1,512,1024]{2,1,0:T(8,128)(2,1)S(1)} %copy-done.28, bf16[8,1024,64,1]{1,2,0,3:T(8,128)(2,1)} %reshape.421), kind=kOutput, calls=%fused_computation.104 | convolution fusion | flops 1078460416 | bytes 4194304 | tf_op jit(solution)/shard_map/rsl,alc->sarc/dot_general | solution.py:102
  139.9 3.0 copy.328
  142.9 2.3 reshape.428
  145.2 34.5 %all_to_all.93 = bf16[64,2,4096]{2,1,0:T(2,128)(2,1)} all-to-all(bf16[64,2,4096]{2,1,0:T(2,128)(2,1)} %reshape.428), channel_id=1, replica_groups=mesh['lat'=64,'lon'=4] {'lat'}, dimensions={0} | all-to-all | bytes 2097152 | tf_op jit(solution)/shard_map/all_to_all | solution.py:107
  179.6 3.8 %reshape.429 = bf16[64,4,2,2,8,64]{5,4,3,2,1,0:T(8,128)(2,1)S(1)} reshape(bf16[64,2,4096]{2,1,0:T(2,128)(2,1)} %all_to_all.93) | data formatting | bytes 2097152
  185.3 2.7 copy.330
  188.0 6.2 %all-to-all-start.2 = ((bf16[1,4,2,512,2,64]{3,5,4,2,0,1:T(8,128)(2,1)}), bf16[1,4,2,512,2,64]{3,5,4,2,0,1:T(8,128)(2,1)S(1)}, u32[]{:S(2)}, u32[]{:S(2)}) async-start(bf16[1,4,2,512,2,64]{3,5,4,2,0,1:T(8,128)(2,1)} %copy.330), calls=%async_computation.2 | async-start | bytes 2097152 | tf_op jit(solution)/shard_map/all_to_all | solution.py:106
  195.2 14.2 %all-to-all-done.2 = bf16[1,4,2,512,2,64]{3,5,4,2,0,1:T(8,128)(2,1)S(1)} async-done(((bf16[1,4,2,512,2,64]{3,5,4,2,0,1:T(8,128)(2,1)}), bf16[1,4,2,512,2,64]{3,5,4,2,0,1:T(8,128)(2,1)S(1)}, u32[]{:S(2)}, u32[]{:S(2)}) %all-to-all-start.2) | async-done | bytes 1048608 | tf_op jit(solution)/shard_map/all_to_all | solution.py:106
  209.4 2.0 convolution_convert_fusion.1
  213.8 2.2 fusion.34
  217.0 32.8 %all_to_all.94 = bf16[1,1,2,512,2,256]{5,4,2,1,0,3:T(2,128)(2,1)} all-to-all(bf16[1,1,2,512,2,256]{5,4,2,1,0,3:T(2,128)(2,1)S(1)} %copy.336), channel_id=1, replica_groups=mesh['lat'=64,'lon'=4] {'lat'}, dimensions={3} | all-to-all | bytes 2097152 | tf_op jit(solution)/shard_map/all_to_all | solution.py:136
  249.8 3.6 %copy.337 = bf16[1,1,2,64,8,2,256]{3,4,5,2,6,1,0:T(8,128)(2,1)S(1)} copy(bf16[1,1,2,64,8,2,256]{6,5,2,4,3,1,0:T(2,128)(2,1)} %bitcast.322) | data formatting | bytes 2097152 | tf_op jit(solution)/shard_map/all_to_all | solution.py:136
  255.1 3.4 %reshape.430 = bf16[4,2,65536]{2,1,0:T(2,128)(2,1)S(1)} reshape(bf16[256,1,2,2,8,64]{5,4,3,2,1,0:T(8,128)(2,1)} %bitcast_bitcast_fusion.1) | data formatting | bytes 2097152
  258.5 20.7 %all_to_all.95 = bf16[4,2,65536]{2,1,0:T(2,128)(2,1)} all-to-all(bf16[4,2,65536]{2,1,0:T(2,128)(2,1)S(1)} %reshape.430), channel_id=1, replica_groups=mesh['lat'=64,'lon'=4] {'lon'}, dimensions={0} | all-to-all | bytes 2097152 | tf_op jit(solution)/shard_map/all_to_all | solution.py:135
  279.2 3.1 reshape.431
  282.3 4.9 %copy.356 = bf16[64,1,2,8,2,4,64]{6,5,3,4,2,0,1:T(4,128)(2,1)} copy(bf16[64,1,2,8,2,4,64]{0,3,4,2,6,5,1:T(8,128)(2,1)S(1)} %bitcast.317) | data formatting | bytes 2097152 | tf_op jit(solution)/shard_map/all_to_all | solution.py:135
  287.2 2.3 copy.339
  289.5 2.4 fusion.36
  292.0 2.6 copy.341
  294.6 2.7 reshape.432
  297.3 5.5 %all-to-all-start.5 = ((bf16[4,2,65536]{2,1,0:T(2,128)(2,1)}), bf16[4,2,65536]{2,1,0:T(2,128)(2,1)}, u32[]{:S(2)}, u32[]{:S(2)}) async-start(bf16[4,2,65536]{2,1,0:T(2,128)(2,1)} %reshape.432), calls=%async_computation.5 | async-start | bytes 2097152 | tf_op jit(solution)/shard_map/all_to_all | solution.py:147
  303.4 2.2 copy.384
  305.5 12.4 %all-to-all-done.5 = bf16[4,2,65536]{2,1,0:T(2,128)(2,1)} async-done(((bf16[4,2,65536]{2,1,0:T(2,128)(2,1)}), bf16[4,2,65536]{2,1,0:T(2,128)(2,1)}, u32[]{:S(2)}, u32[]{:S(2)}) %all-to-all-start.5) | async-done | bytes 1048608 | tf_op jit(solution)/shard_map/all_to_all | solution.py:147
  317.9 3.1 reshape.433
  321.0 2.6 copy.342
  323.6 4.0 %copy.383 = f32[32,8,8,256]{3,1,2,0:T(8,128)} copy(f32[32,8,8,256]{3,2,1,0:T(8,128)} %bitcast.321) | data formatting | bytes 4194304
  327.6 5.0 %fusion.9 = bf16[2048,256]{1,0:T(8,128)(2,1)} fusion(bf16[512,256]{1,0:T(8,128)(2,1)} %param.17, bf16[2048,256]{1,0:T(8,128)(2,1)S(1)} %bitcast.326, bf16[256,512]{1,0:T(8,128)(2,1)} %param.16, f32[2048,256]{0,1:T(8,128)} %bitcast.330, f32[2048,256]{0,1:T(8,128)S(1)} %bitcast.328), kind=kOutput, calls=%fused_computation.16 | convolution fusion | flops 1089994752 | bytes 6815744 | tf_op jit(solution)/shard_map/dot_general | solution.py:155
  (157 shorter events, 38.8 us)
Async XLA Ops:
  0.0 86.7 %copy-start = (bf16[4,2,128,128]{3,2,1,0:T(8,128)(2,1)S(1)}, bf16[4,2,128,128]{3,2,1,0:T(8,128)(2,1)}, u32[]{:S(2)}) copy-start(bf16[4,2,128,128]{3,2,1,0:T(8,128)(2,1)} %param.12) | copy-start | bytes 786436
  0.0 17.8 %copy-start.21 = (bf16[8,256,256]{2,1,0:T(8,128)(2,1)S(1)}, bf16[8,256,256]{2,1,0:T(8,128)(2,1)}, u32[]{:S(2)}) copy-start(bf16[8,256,256]{2,1,0:T(8,128)(2,1)} %param.9) | copy-start | bytes 3145732
  1.9 15.8 %collective-permute-start = (bf16[2,256,256]{2,1,0:T(8,128)(2,1)S(1)}, bf16[2,256,256]{2,1,0:T(8,128)(2,1)S(1)}, u32[]{:S(2)}, u32[]{:S(2)}) collective-permute-start(bf16[2,256,256]{2,1,0:T(8,128)(2,1)S(1)} %get-tuple-element.33), channel_id=1, source_target_pairs={{0,4},{4,8},{8,12},{12,16},{16,20},{20,24},{24,28},{28,32},{32,36}... | collective-permute-start | bytes 786440 | tf_op jit(solution)/shard_map/ppermute | solution.py:16
  4.0 13.8 %collective-permute-start.1 = (bf16[2,256,256]{2,1,0:T(8,128)(2,1)}, bf16[2,256,256]{2,1,0:T(8,128)(2,1)S(1)}, u32[]{:S(2)}, u32[]{:S(2)}) collective-permute-start(bf16[2,256,256]{2,1,0:T(8,128)(2,1)} %get-tuple-element.32), channel_id=1, source_target_pairs={{4,0},{8,4},{12,8},{16,12},{20,16},{24,20},{28,24},{32,28},{36,32}... | collective-permute-start | bytes 786440 | tf_op jit(solution)/shard_map/ppermute | solution.py:18
  17.7 4.5 %copy-start.39 = (f32[4,8]{1,0:T(4,128)S(1)}, f32[4,8]{1,0:T(4,128)}, u32[]{:S(2)}) copy-start(f32[4,8]{1,0:T(4,128)} %get-tuple-element.36) | copy-start | bytes 388
  17.7 5.1 %copy-start.38 = (f32[4,8]{1,0:T(4,128)S(1)}, f32[4,8]{1,0:T(4,128)}, u32[]{:S(2)}) copy-start(f32[4,8]{1,0:T(4,128)} %get-tuple-element.54) | copy-start | bytes 388
  17.7 5.8 %copy-start.37 = (f32[4,8]{1,0:T(4,128)S(1)}, f32[4,8]{1,0:T(4,128)}, u32[]{:S(2)}) copy-start(f32[4,8]{1,0:T(4,128)} %get-tuple-element.53) | copy-start | bytes 388
  17.7 6.5 %copy-start.36 = (f32[4,8]{1,0:T(4,128)S(1)}, f32[4,8]{1,0:T(4,128)}, u32[]{:S(2)}) copy-start(f32[4,8]{1,0:T(4,128)} %get-tuple-element.52) | copy-start | bytes 388
  17.7 7.1 %copy-start.35 = (f32[4,8]{1,0:T(4,128)S(1)}, f32[4,8]{1,0:T(4,128)}, u32[]{:S(2)}) copy-start(f32[4,8]{1,0:T(4,128)} %get-tuple-element.51) | copy-start | bytes 388
  17.7 7.8 %copy-start.34 = (f32[4,8]{1,0:T(4,128)S(1)}, f32[4,8]{1,0:T(4,128)}, u32[]{:S(2)}) copy-start(f32[4,8]{1,0:T(4,128)} %get-tuple-element.50) | copy-start | bytes 388
  17.7 8.5 %copy-start.33 = (f32[4,8]{1,0:T(4,128)S(1)}, f32[4,8]{1,0:T(4,128)}, u32[]{:S(2)}) copy-start(f32[4,8]{1,0:T(4,128)} %get-tuple-element.49) | copy-start | bytes 388
  17.9 11.0 %collective-permute-start.2 = (bf16[12,2,256]{2,1,0:T(2,128)(2,1)S(1)}, bf16[12,2,256]{2,1,0:T(2,128)(2,1)S(1)}, u32[]{:S(2)}, u32[]{:S(2)}) collective-permute-start(bf16[12,2,256]{2,1,0:T(2,128)(2,1)S(1)} %get-tuple-element.30), channel_id=1, source_target_pairs={{0,1},{1,2},{2,3},{3,0},{4,5},{5,6},{6,7},{7,4},{8,9},{9,10},{10,1... | collective-permute-start | bytes 36872 | tf_op jit(solution)/shard_map/ppermute | solution.py:16
  21.6 7.4 %collective-permute-start.3 = (bf16[12,2,256]{2,1,0:T(2,128)(2,1)S(1)}, bf16[12,2,256]{2,1,0:T(2,128)(2,1)S(1)}, u32[]{:S(2)}, u32[]{:S(2)}) collective-permute-start(bf16[12,2,256]{2,1,0:T(2,128)(2,1)S(1)} %get-tuple-element.31), channel_id=1, source_target_pairs={{1,0},{2,1},{3,2},{0,3},{5,4},{6,5},{7,6},{4,7},{9,8},{10,9},{11,1... | collective-permute-start | bytes 36872 | tf_op jit(solution)/shard_map/ppermute | solution.py:18
  47.2 2.3 copy-start.17
  47.2 3.0 copy-start.18
  50.2 2.7 copy-start.15
  50.2 3.7 %copy-start.16 = (f32[8,32,2,8,128]{4,3,2,1,0:T(8,128)S(1)}, f32[8,32,2,8,128]{4,3,2,1,0:T(8,128)}, u32[]{:S(2)}) copy-start(f32[8,32,2,8,128]{4,3,2,1,0:T(8,128)} %get-tuple-element.19) | copy-start | bytes 6291460
  53.9 2.7 copy-start.13
  53.9 3.7 %copy-start.14 = (f32[8,32,2,8,128]{4,3,2,1,0:T(8,128)S(1)}, f32[8,32,2,8,128]{4,3,2,1,0:T(8,128)}, u32[]{:S(2)}) copy-start(f32[8,32,2,8,128]{4,3,2,1,0:T(8,128)} %get-tuple-element.17) | copy-start | bytes 6291460
  57.7 2.7 copy-start.11
  57.7 3.7 %copy-start.12 = (f32[8,32,2,8,128]{4,3,2,1,0:T(8,128)S(1)}, f32[8,32,2,8,128]{4,3,2,1,0:T(8,128)}, u32[]{:S(2)}) copy-start(f32[8,32,2,8,128]{4,3,2,1,0:T(8,128)} %get-tuple-element.15) | copy-start | bytes 6291460
  61.4 2.7 copy-start.9
  61.4 3.7 %copy-start.10 = (f32[8,32,2,8,128]{4,3,2,1,0:T(8,128)S(1)}, f32[8,32,2,8,128]{4,3,2,1,0:T(8,128)}, u32[]{:S(2)}) copy-start(f32[8,32,2,8,128]{4,3,2,1,0:T(8,128)} %get-tuple-element.13) | copy-start | bytes 6291460
  65.2 2.7 copy-start.7
  65.2 3.7 %copy-start.8 = (f32[8,32,2,8,128]{4,3,2,1,0:T(8,128)S(1)}, f32[8,32,2,8,128]{4,3,2,1,0:T(8,128)}, u32[]{:S(2)}) copy-start(f32[8,32,2,8,128]{4,3,2,1,0:T(8,128)} %get-tuple-element.11) | copy-start | bytes 6291460
  68.9 2.7 copy-start.5
  68.9 3.7 %copy-start.6 = (f32[8,32,2,8,128]{4,3,2,1,0:T(8,128)S(1)}, f32[8,32,2,8,128]{4,3,2,1,0:T(8,128)}, u32[]{:S(2)}) copy-start(f32[8,32,2,8,128]{4,3,2,1,0:T(8,128)} %get-tuple-element.9) | copy-start | bytes 6291460
  72.6 2.7 copy-start.3
  72.6 3.7 %copy-start.4 = (f32[8,32,2,8,128]{4,3,2,1,0:T(8,128)S(1)}, f32[8,32,2,8,128]{4,3,2,1,0:T(8,128)}, u32[]{:S(2)}) copy-start(f32[8,32,2,8,128]{4,3,2,1,0:T(8,128)} %get-tuple-element.7) | copy-start | bytes 6291460
  84.0 2.7 copy-start.24
  84.0 3.7 %copy-start.25 = (f32[8,256,2,128]{3,1,0,2:T(8,128)S(1)}, f32[8,256,2,128]{3,1,0,2:T(8,128)}, u32[]{:S(2)}) copy-start(f32[8,256,2,128]{3,1,0,2:T(8,128)} %get-tuple-element.79) | copy-start | bytes 6291460
  84.0 3.7 %copy-start.40 = (f32[4,8]{0,1:T(8,128)S(1)}, f32[4,8]{0,1:T(8,128)}, u32[]{:S(2)}) copy-start(f32[4,8]{0,1:T(8,128)} %copy.273) | copy-start | bytes 388
  84.0 3.7 %copy-start.41 = (f32[4,8]{0,1:T(8,128)S(1)}, f32[4,8]{0,1:T(8,128)}, u32[]{:S(2)}) copy-start(f32[4,8]{0,1:T(8,128)} %copy.287) | copy-start | bytes 388
  84.0 3.7 %copy-start.42 = (f32[4,8]{0,1:T(8,128)S(1)}, f32[4,8]{0,1:T(8,128)}, u32[]{:S(2)}) copy-start(f32[4,8]{0,1:T(8,128)} %copy.289) | copy-start | bytes 388
  84.0 3.7 %copy-start.43 = (f32[4,8]{0,1:T(8,128)S(1)}, f32[4,8]{0,1:T(8,128)}, u32[]{:S(2)}) copy-start(f32[4,8]{0,1:T(8,128)} %copy.291) | copy-start | bytes 388
  84.0 3.7 %copy-start.44 = (f32[4,8]{0,1:T(8,128)S(1)}, f32[4,8]{0,1:T(8,128)}, u32[]{:S(2)}) copy-start(f32[4,8]{0,1:T(8,128)} %copy.293) | copy-start | bytes 388
  84.0 3.7 %copy-start.45 = (f32[4,8]{0,1:T(8,128)S(1)}, f32[4,8]{0,1:T(8,128)}, u32[]{:S(2)}) copy-start(f32[4,8]{0,1:T(8,128)} %copy.295) | copy-start | bytes 388
  84.0 3.7 %copy-start.46 = (f32[4,8]{0,1:T(8,128)S(1)}, f32[4,8]{0,1:T(8,128)}, u32[]{:S(2)}) copy-start(f32[4,8]{0,1:T(8,128)} %copy.297) | copy-start | bytes 388
  84.0 3.7 %copy-start.47 = (f32[4,8]{0,1:T(8,128)S(1)}, f32[4,8]{0,1:T(8,128)}, u32[]{:S(2)}) copy-start(f32[4,8]{0,1:T(8,128)} %copy.299) | copy-start | bytes 388
  112.1 6.5 %copy-start.32 = (s32[512]{0:T(512)S(1)}, s32[512]{0:T(512)}, u32[]{:S(2)}) copy-start(s32[512]{0:T(512)} %param.13) | copy-start | bytes 6148
  113.7 20.0 %all-to-all-start = ((bf16[8,256,256]{1,0,2:T(8,128)(2,1)}), bf16[8,256,256]{1,0,2:T(8,128)(2,1)S(1)}, u32[]{:S(2)}, u32[]{:S(2)}) async-start(bf16[8,256,256]{1,0,2:T(8,128)(2,1)} %copy.325), calls=%async_computation | async-start | bytes 2097152 | tf_op jit(solution)/shard_map/all_to_all | solution.py:100
  185.3 9.1 %copy-start.29 = (bf16[2,256,256]{2,1,0:T(8,128)(2,1)S(1)}, bf16[2,256,256]{2,1,0:T(8,128)(2,1)}, u32[]{:S(2)}) copy-start(bf16[2,256,256]{2,1,0:T(8,128)(2,1)} %param.15) | copy-start | bytes 786436
  188.0 21.3 %all-to-all-start.2 = ((bf16[1,4,2,512,2,64]{3,5,4,2,0,1:T(8,128)(2,1)}), bf16[1,4,2,512,2,64]{3,5,4,2,0,1:T(8,128)(2,1)S(1)}, u32[]{:S(2)}, u32[]{:S(2)}) async-start(bf16[1,4,2,512,2,64]{3,5,4,2,0,1:T(8,128)(2,1)} %copy.330), calls=%async_computation.2 | async-start | bytes 2097152 | tf_op jit(solution)/shard_map/all_to_all | solution.py:106
  287.2 2.3 copy-start.27
  297.3 20.6 %all-to-all-start.5 = ((bf16[4,2,65536]{2,1,0:T(2,128)(2,1)}), bf16[4,2,65536]{2,1,0:T(2,128)(2,1)}, u32[]{:S(2)}, u32[]{:S(2)}) async-start(bf16[4,2,65536]{2,1,0:T(2,128)(2,1)} %reshape.432), calls=%async_computation.5 | async-start | bytes 2097152 | tf_op jit(solution)/shard_map/all_to_all | solution.py:147
  323.6 4.0 %copy-start.22 = (bf16[8,256,256]{2,1,0:T(8,128)(2,1)S(1)}, bf16[8,256,256]{2,1,0:T(8,128)(2,1)}, u32[]{:S(2)}) copy-start(bf16[8,256,256]{2,1,0:T(8,128)(2,1)} %param.9) | copy-start | bytes 3145732
  323.6 4.0 %copy-start.23 = (f32[32,8,8,256]{3,1,2,0:T(8,128)S(1)}, f32[32,8,8,256]{3,1,2,0:T(8,128)}, u32[]{:S(2)}) copy-start(f32[32,8,8,256]{3,1,2,0:T(8,128)} %copy.384) | copy-start | bytes 6291460
  327.6 5.0 %copy-start.1 = (bf16[4,2,128,128]{3,2,1,0:T(8,128)(2,1)S(1)}, bf16[4,2,128,128]{3,2,1,0:T(8,128)(2,1)}, u32[]{:S(2)}) copy-start(bf16[4,2,128,128]{3,2,1,0:T(8,128)(2,1)} %param.12) | copy-start | bytes 786436
  (7 other events, 12.0 us)
where the time goes:
time: 337 us; the launch traced here: 333 us
  local copies, waits for them, and re-layouts  112 us (33%)
  blocking collectives  87.9 us (26%)
  matrix products  40.4 us (12%)
  waiting for transfers between devices  34.2 us (10%)
  starting transfers between devices  30 us (9%)
  other arithmetic  27.9 us (8%)
    unnamed x110, local copies, waits for them, and re-layouts  39.9 us
    all_to_all x1, blocking collectives, shards(): lax.all_to_all(spectra, 'lat', split_axis=0, concat_axis=3, tiled=True)  34.5 us
    all_to_all x1, blocking collectives, shards(): lax.all_to_all(sectioned, 'lat', split_axis=3, concat_axis=0, tiled=True)  32.8 us
    mul x13, local copies, waits for them, and re-layouts, disco_layer(): running = running + scales[:, :, None, None] * window[None]  30.9 us
    dot_general x1, matrix products, disco_layer(): jnp.einsum('kajgi,kgio->ajgo', response, disco_weight, preferred_element_...  24.3 us
    all_to_all x1, blocking collectives, shards(): lax.all_to_all(lax.all_to_all(sectioned, 'lat', split_axis=3, concat_axis...  20.7 us
    unnamed x2, other arithmetic  14.6 us
    all_to_all x1, waiting for transfers between devices, shards(): lax.all_to_all(lax.all_to_all(spectra, 'lat', split_axis=0, concat_axis=3...  14.2 us
  transfers between devices with their start and end apart: 7, of which 4 were waited for; matrix products, arithmetic and copies ran while one was open for 7% of the time, Pallas kernels for 0%

commit v1 on v0

v1 whole, which is shorter than its diff:
```python
import math

import jax
import jax.numpy as jnp
import numpy as np
from jax import lax
from jax.experimental import pallas as pl
from jax.experimental.pallas import tpu as pltpu
from jax.sharding import PartitionSpec as P

MESH = pl.DeviceIdType.MESH
BF = jnp.bfloat16
F32 = jnp.float32
I32 = jnp.int32

LATS = 64
LONS = 4
NLON = 1024
MODES = 512
ROWS = 8
COLS = 256
CH = 256
HALF = 128
WIN = 96
TILE = 64
RIM = 16


def wave_tables():
    q = (np.arange(MODES)[:, None] * np.arange(NLON)[None, :]) % NLON
    phase = 2.0 * np.pi * q / NLON
    waves = np.stack([np.cos(phase), -np.sin(phase)]) / math.sqrt(NLON)
    return waves


def dot(a, b):
    return jnp.dot(a, b, preferred_element_type=F32)


def gelu(x):
    return jax.nn.gelu(x, approximate=True)


def rows_of(start, size):
    return pl.ds(pl.multiple_of(start, 16), size)


def half_of(index):
    return pl.ds(pl.multiple_of(index * HALF, HALF), HALF)


def swing(k):
    return ((k + 1) // 2) * (2 * (k % 2) - 1)


def layer(
    field, basis, quad, mix_w, keys, modes, legendre, filt, inner, outer, waves, waves_t,
    out,
    ext, wdisco, tab, tab_t, wav, wav_t, band, diag, sel, dsend, full, ssend, srecv, spec, leg, leg_t,
    fmat, ssend2, srecv2, zed, psend, precv, perm_a, perm_at, perm_b, perm_bt, w_in, w_out, w_filt,
    load_sem, halo_send, halo_recv, d_send, d_recv, s_send, s_recv, b_send, b_recv, p_send, p_recv,
):
    lat = lax.axis_index("lat")
    lon = lax.axis_index("lon")
    me = lat * LONS + lon
    lat_y = lat % 4
    lat_xz = lat // 4
    my_h = lon // 2
    my_g = lon % 2
    north = (lat + LATS - 1) % LATS
    south = (lat + 1) % LATS
    west = (lon + LONS - 1) % LONS
    east = (lon + 1) % LONS
    across = (lon + 2) % LONS

    barrier = pltpu.get_barrier_semaphore()

    def greet(n, carry):
        to = (me + swing(n) + 256) % 256
        pl.semaphore_signal(
            barrier, inc=1, device_id=(to // LONS, to % LONS), device_id_type=MESH
        )
        return carry

    lax.fori_loop(1, 256, greet, 0)

    loads = [
        pltpu.make_async_copy(field, ext.at[2 : 2 + ROWS, RIM : RIM + COLS, :], load_sem.at[0]),
        pltpu.make_async_copy(waves, wav, load_sem.at[1]),
        pltpu.make_async_copy(waves_t, wav_t, load_sem.at[2]),
        pltpu.make_async_copy(legendre, leg, load_sem.at[3]),
        pltpu.make_async_copy(inner, w_in, load_sem.at[4]),
        pltpu.make_async_copy(outer, w_out, load_sem.at[5]),
        pltpu.make_async_copy(filt, w_filt, load_sem.at[6]),
    ]
    for load in loads:
        load.start()
    for g in range(2):
        for k in range(4):
            pltpu.make_async_copy(
                mix_w.at[k, g], wdisco.at[g, k * HALF : (k + 1) * HALF, :], load_sem.at[7]
            ).start()

    row = lax.broadcasted_iota(I32, (256, 256), 0)
    col = lax.broadcasted_iota(I32, (256, 256), 1)

    def sent(n):
        return ((n // 4) % 4) * 64 + (n % 2) * 32 + (n // 16) * 2 + (n // 2) % 2

    def gathered(n):
        return ((n % 64) // 4) * 16 + (n % 4) * 4 + (n // 128) * 2 + (n // 64) % 2

    perm_a[...] = (col == sent(row)).astype(F32).astype(BF)
    perm_at[...] = (row == sent(col)).astype(F32).astype(BF)
    perm_b[...] = (col == gathered(row)).astype(F32).astype(BF)
    perm_bt[...] = (row == gathered(col)).astype(F32).astype(BF)

    point = lax.broadcasted_iota(I32, (25, 512), 0)
    lane25 = lax.broadcasted_iota(I32, (25, 512), 1)
    lane8 = lax.broadcasted_iota(I32, (8, 512), 1)
    lat_row = lat * ROWS + lax.broadcasted_iota(I32, (8, 512), 0) + lane8 // WIN - 2
    inside = (lat_row >= 0) & (lat_row < LATS * ROWS) & (lane8 < 5 * WIN)
    quads = quad[...]
    bases = basis[...].astype(F32).astype(BF)
    for dx in range(5):
        pick = (point == 5 * (lane25 // WIN) + dx).astype(F32).astype(BF)
        weight = jnp.where(inside, dot(quads, pick), 0.0)
        kind = dot(bases, pick)
        for k in range(4):
            sel[5 * k + dx] = jnp.where(kind == float(k), weight, 0.0)
    lane64 = lax.broadcasted_iota(I32, (TILE, 512), 1)
    diag[...] = jnp.where(
        lane64 < 5 * WIN,
        lane64 % WIN - (RIM - 2) - lax.broadcasted_iota(I32, (TILE, 512), 0),
        -1000,
    )

    pl.semaphore_wait(barrier, 255)

    top, bottom = slice(0, 2), slice(ROWS - 2, ROWS)
    left, right = slice(0, RIM), slice(COLS - RIM, COLS)
    here_rows, here_cols = slice(2, 2 + ROWS), slice(RIM, RIM + COLS)
    above, below = slice(0, 2), slice(ROWS + 2, ROWS + 4)
    before, after = slice(0, RIM), slice(RIM + COLS, 2 * RIM + COLS)
    whole = slice(None)
    plan = [
        ((south, lon), (bottom, whole), (above, here_cols)),
        ((north, lon), (top, whole), (below, here_cols)),
        ((lat, east), (whole, right), (here_rows, before)),
        ((lat, west), (whole, left), (here_rows, after)),
        ((south, east), (bottom, right), (above, before)),
        ((south, west), (bottom, left), (above, after)),
        ((north, east), (top, right), (below, before)),
        ((north, west), (top, left), (below, after)),
    ]
    rims = []
    for n, (peer, (sr, sc), (dr, dc)) in enumerate(plan):
        rims.append(
            pltpu.make_async_remote_copy(
                field.at[sr, sc, :], ext.at[dr, dc, :], halo_send.at[n], halo_recv.at[n],
                device_id=peer, device_id_type=MESH,
            )
        )
    for rim in rims:
        rim.start()

    key_rows = keys[...].astype(F32)
    key_cols = jnp.transpose(
        jnp.concatenate([key_rows, jnp.zeros((HALF - 8, HALF), F32)], axis=0)
    ).astype(I32)
    loads[1].wait()
    for y in range(4):
        hot = (
            (lax.broadcasted_iota(I32, (HALF, MODES), 1) == key_cols[:, y : y + 1])
            .astype(F32)
            .astype(BF)
        )
        for r in range(2):
            tab[(2 * y + r) * HALF : (2 * y + r + 1) * HALF, :] = dot(hot, wav[r]).astype(BF)

    loads[0].wait()
    pltpu.make_async_copy(wdisco, wdisco, load_sem.at[7]).wait()
    for rim in rims:
        rim.wait()

    def conv_row(a, carry):
        shift = diag[...]
        for k in range(4):
            values = jnp.zeros((TILE, 512), F32)
            for dx in range(5):
                values = jnp.where(shift == dx, sel[5 * k + dx, pl.ds(a, 1), :], values)
            band[k * TILE : (k + 1) * TILE, :] = values.astype(BF)
        parts = [[], []]
        for tile in range(COLS // TILE):
            j = tile * TILE
            window = jnp.concatenate(
                [ext[a + dy, j : j + WIN, :] for dy in range(5)] + [ext[a, j : j + 32, :]], axis=0
            )
            response = dot(band[...], window).astype(BF)
            for g in range(2):
                parts[g].append(
                    jnp.concatenate(
                        [
                            response[k * TILE : (k + 1) * TILE, g * HALF : (g + 1) * HALF]
                            for k in range(4)
                        ],
                        axis=1,
                    )
                )
        for g in range(2):
            mixed = dot(jnp.concatenate(parts[g], axis=0), wdisco[g]).astype(BF)
            dsend[(a // 4) * 2 + g, :, half_of(a % 4)] = mixed
        return carry

    def d_copy(part):
        return pltpu.make_async_remote_copy(
            dsend.at[part], full.at[rows_of(lon * COLS, COLS), :], d_send, d_recv,
            device_id=(lat, part), device_id_type=MESH,
        )

    def d_start(part):
        @pl.when(part != lon)
        def _():
            d_copy(part).start()

        @pl.when(part == lon)
        def _():
            pltpu.make_async_copy(
                dsend.at[part], full.at[rows_of(lon * COLS, COLS), :], d_recv
            ).start()

    lax.fori_loop(0, 4, conv_row, 0)
    d_start(0)
    d_start(1)
    lax.fori_loop(4, 8, conv_row, 0)
    d_start(2)
    d_start(3)

    loads[3].wait()
    for t in range(2):
        least = modes[me * 2 + t]
        allowed = lax.broadcasted_iota(I32, (MODES, MODES), 0) >= least
        masked = jnp.where(allowed, leg[t].astype(F32), 0.0)
        leg[t] = masked.astype(BF)
        leg_t[t] = jnp.transpose(masked).astype(BF)
    loads[6].wait()
    fmat[0:CH, 0:CH] = w_filt[0]
    fmat[0:CH, CH : 2 * CH] = w_filt[1]
    fmat[CH : 2 * CH, 0:CH] = -w_filt[1]
    fmat[CH : 2 * CH, CH : 2 * CH] = w_filt[0]

    pltpu.make_async_copy(full, full, d_recv).wait()
    my_pos = lat_xz * 4 + lon

    def s_block(i, carry):
        y = (lat_y + i) % 4
        waved = dot(tab[rows_of(y * 256, 256), :], full[...]).astype(BF)
        for q in range(4):
            stacked = jnp.concatenate(
                [
                    waved[r * HALF + q * 32 : r * HALF + q * 32 + 32, a * HALF : (a + 1) * HALF]
                    for a in range(4)
                    for r in range(2)
                ],
                axis=0,
            )
            ssend[rows_of((y * 4 + q) * 256, 256), :] = dot(perm_a[...], stacked).astype(BF)

        def one(n, c):
            pos = (my_pos + swing(n) + 64) % 64
            s_copy(y, pos).start()
            return c

        def s_copy(y, pos):
            return pltpu.make_async_remote_copy(
                ssend.at[rows_of((y * 64 + pos) * 16, 16), :],
                srecv.at[rows_of((lat * 2 + my_h) * 16, 16), half_of(my_g)],
                s_send, s_recv,
                device_id=((pos // 4) * 4 + y, pos % 4), device_id_type=MESH,
            )

        @pl.when(i == 0)
        def _():
            pltpu.make_async_copy(
                ssend.at[rows_of((y * 64 + my_pos) * 16, 16), :],
                srecv.at[rows_of((lat * 2 + my_h) * 16, 16), half_of(my_g)],
                s_recv,
            ).start()

        @pl.when(i != 0)
        def _():
            s_copy(y, my_pos).start()

        lax.fori_loop(1, 64, one, 0)
        return carry

    lax.fori_loop(0, 4, s_block, 0)

    loads[2].wait()
    for y in range(4):
        hot = (
            (lax.broadcasted_iota(I32, (MODES, HALF), 0) == keys[y : y + 1, :])
            .astype(F32)
            .astype(BF)
        )
        for r in range(2):
            tab_t[:, (2 * y + r) * HALF : (2 * y + r + 1) * HALF] = dot(wav_t[r], hot).astype(BF)

    pltpu.make_async_copy(srecv, srecv, s_recv).wait()

    for b in range(8):
        turned = dot(perm_b[...], srecv[b * 256 : (b + 1) * 256, :]).astype(BF)
        for t in range(2):
            for r in range(2):
                spec[t, b * 64 : (b + 1) * 64, r * CH : (r + 1) * CH] = turned[
                    t * 128 + r * 64 : t * 128 + r * 64 + 64, :
                ]

    for t in range(2):
        coeffs = dot(leg[t], spec[t]).astype(BF)
        filtered = dot(coeffs, fmat[...]).astype(BF)
        back = dot(leg_t[t], filtered)
        scale = jnp.where(modes[me * 2 + t] == 0, 1.0, 2.0).astype(F32)
        spec[t] = (back * scale).astype(BF)

    for b in range(8):
        stacked = jnp.concatenate(
            [
                spec[t, b * 64 : (b + 1) * 64, r * CH : (r + 1) * CH]
                for t in range(2)
                for r in range(2)
            ],
            axis=0,
        )
        ssend2[b * 256 : (b + 1) * 256, :] = dot(perm_bt[...], stacked).astype(BF)

    back_row = (lat_y * 64 + my_pos) * 16

    def b_one(n, c):
        to = (me + swing(n) + 256) % 256
        pltpu.make_async_remote_copy(
            ssend2.at[rows_of((to // 2) * 16, 16), half_of(to % 2)],
            srecv2.at[rows_of(back_row, 16), :],
            b_send, b_recv,
            device_id=(to // 4, to % 4), device_id_type=MESH,
        ).start()
        return c

    pltpu.make_async_copy(
        ssend2.at[rows_of((me // 2) * 16, 16), half_of(my_g)],
        srecv2.at[rows_of(back_row, 16), :],
        b_recv,
    ).start()
    lax.fori_loop(1, 256, b_one, 0)
    loads[4].wait()
    loads[5].wait()
    pltpu.make_async_copy(srecv2, srecv2, b_recv).wait()

    for n in range(16):
        turned = dot(perm_at[...], srecv2[n * 256 : (n + 1) * 256, :]).astype(BF)
        for a in range(4):
            for r in range(2):
                start = (n // 4) * 256 + r * HALF + (n % 4) * 32
                zed[start : start + 32, a * HALF : (a + 1) * HALF] = turned[
                    a * 64 + r * 32 : a * 64 + r * 32 + 32, :
                ]

    def p_block(i, carry):
        to = (lon + 1 + i) % LONS
        part = rows_of(to * COLS, COLS)
        psend[part, :] = dot(tab_t[part, :], zed[...]).astype(BF)

        @pl.when(i != 3)
        def _():
            pltpu.make_async_remote_copy(
                psend.at[part, :], precv.at[lon], p_send, p_recv,
                device_id=(lat, to), device_id_type=MESH,
            ).start()

        @pl.when(i == 3)
        def _():
            pltpu.make_async_copy(psend.at[part, :], precv.at[lon], p_recv).start()

        return carry

    lax.fori_loop(0, 4, p_block, 0)
    pltpu.make_async_copy(precv, precv, p_recv).wait()

    def mlp_row(a, carry):
        h = a // 4
        lanes = half_of(a % 4)
        mixed = jnp.concatenate(
            [
                gelu(precv[2 * h + g, :, lanes].astype(F32) + dsend[2 * h + g, :, lanes].astype(F32))
                for g in range(2)
            ],
            axis=1,
        ).astype(BF)
        hidden = gelu(dot(mixed, w_in[...])).astype(BF)
        result = ext[a + 2, RIM : RIM + COLS, :].astype(F32) + dot(hidden, w_out[...])
        out[a] = result.astype(BF)
        return carry

    lax.fori_loop(0, 8, mlp_row, 0)

    pltpu.make_async_copy(dsend.at[0:3], dsend.at[0:3], d_send).wait()
    pltpu.make_async_copy(ssend.at[0:4080], ssend.at[0:4080], s_send).wait()
    pltpu.make_async_copy(srecv2.at[0:4080], srecv2.at[0:4080], b_send).wait()
    pltpu.make_async_copy(psend.at[0 : 3 * COLS], psend.at[0 : 3 * COLS], p_send).wait()


def shards(
    grid_field, basis_index, quad_weight, disco_weight, mode_order, legendre, filter_weight,
    inner_weight, outer_weight,
):
    table = wave_tables()
    waves = jnp.asarray(table, BF)
    waves_t = jnp.asarray(np.swapaxes(table, 1, 2), BF)
    keys = mode_order.reshape(16, 4, 8).transpose(1, 0, 2).reshape(4, HALF)
    keys = jnp.concatenate([keys, keys], axis=0)
    vmem = pl.BlockSpec(memory_space=pltpu.VMEM)
    smem = pl.BlockSpec(memory_space=pltpu.SMEM)
    anywhere = pl.BlockSpec(memory_space=pl.ANY)
    dma = pltpu.SemaphoreType.DMA
    scratch = [
        pltpu.VMEM((ROWS + 4, COLS + 2 * RIM, CH), BF),
        pltpu.VMEM((2, 512, HALF), BF),
        pltpu.VMEM((1024, NLON), BF),
        pltpu.VMEM((NLON, 1024), BF),
        pltpu.VMEM((2, MODES, NLON), BF),
        pltpu.VMEM((2, NLON, MODES), BF),
        pltpu.VMEM((4 * TILE, 512), BF),
        pltpu.VMEM((TILE, 512), I32),
        pltpu.VMEM((20, 8, 512), F32),
        pltpu.VMEM((4, COLS, 512), BF),
        pltpu.VMEM((NLON, 512), BF),
        pltpu.VMEM((4096, HALF), BF),
        pltpu.VMEM((2048, CH), BF),
        pltpu.VMEM((2, 512, 512), BF),
        pltpu.VMEM((2, 512, 512), BF),
        pltpu.VMEM((2, 512, 512), BF),
        pltpu.VMEM((512, 512), BF),
        pltpu.VMEM((2048, CH), BF),
        pltpu.VMEM((4096, HALF), BF),
        pltpu.VMEM((1024, 512), BF),
        pltpu.VMEM((NLON, 512), BF),
        pltpu.VMEM((4, COLS, 512), BF),
        pltpu.VMEM((256, 256), BF),
        pltpu.VMEM((256, 256), BF),
        pltpu.VMEM((256, 256), BF),
        pltpu.VMEM((256, 256), BF),
        pltpu.VMEM((CH, 512), BF),
        pltpu.VMEM((512, CH), BF),
        pltpu.VMEM((2, CH, CH), BF),
        dma((8,)),
        dma((8,)),
        dma((8,)),
        dma, dma, dma, dma, dma, dma, dma, dma,
    ]
    return pl.pallas_call(
        layer,
        out_shape=jax.ShapeDtypeStruct((ROWS, COLS, CH), BF),
        in_specs=[
            anywhere, vmem, vmem, anywhere, vmem, smem, anywhere, anywhere, anywhere, anywhere,
            anywhere, anywhere,
        ],
        out_specs=vmem,
        scratch_shapes=scratch,
        compiler_params=pltpu.CompilerParams(
            collective_id=0, has_side_effects=True, vmem_limit_bytes=56 * 1024 * 1024
        ),
        name="layer",
    )(
        grid_field, basis_index, quad_weight, disco_weight, keys, mode_order, legendre,
        filter_weight, inner_weight, outer_weight, waves, waves_t,
    )


def solution(mesh):
    in_specs = (
        P("lat", "lon", None),
        P("lat", None),
        P("lat", None),
        P(),
        P(),
        P(("lat", "lon"), None, None),
        P(),
        P(),
        P(),
    )
    out_specs = P("lat", "lon", None)
    return jax.shard_map(shards, mesh=mesh, in_specs=in_specs, out_specs=out_specs, check_vma=False)
```

time: 337 us -> 127 us (0.38); the launches traced: 333 us -> 127 us
  Pallas kernels: 0 us -> 123 us
  local copies, waits for them, and re-layouts: 112 us -> 3.13 us
  blocking collectives: 87.9 us -> 0 us
  matrix products: 40.4 us -> 0 us
  waiting for transfers between devices: 34.2 us -> 0 us
  starting transfers between devices: 30 us -> 0 us
  other arithmetic: 27.9 us -> 0.61 us
    pallas_call x0 -> x1, Pallas kernels: none -> 123 us  [shards(): pl.pallas_call(layer, out_shape=jax.ShapeDtypeStruct((ROWS, COLS, CH), BF...]
    all_to_all x3 -> x0, blocking collectives: 87.9 us -> none  [the longest x1 34.5 us: shards(): lax.all_to_all(spectra, 'lat', split_axis=0, concat_axis=3, tiled=True)]
    dot_general x7 -> x0, matrix products: 40.4 us -> none  [the longest x1 24.3 us: disco_layer(): jnp.einsum('kajgi,kgio->ajgo', response, disco_weight, preferred_element_...]
    unnamed x110 -> x1, local copies, waits for them, and re-layouts: 39.9 us -> 2.26 us
    mul x13 -> x0, local copies, waits for them, and re-layouts: 30.9 us -> none  [disco_layer(): running = running + scales[:, :, None, None] * window[None]]
    all_to_all x3 -> x0, waiting for transfers between devices: 30.3 us -> none  [the longest x1 14.2 us: shards(): lax.all_to_all(lax.all_to_all(spectra, 'lat', split_axis=0, concat_axis=3...]
    all_to_all x8 -> x0, local copies, waits for them, and re-layouts: 17.9 us -> none  [the longest x2 7.21 us: shards(): lax.all_to_all(lax.all_to_all(sectioned, 'lat', split_axis=3, concat_axis...]
    all_to_all x3 -> x0, starting transfers between devices: 16.6 us -> none  [the longest x1 6.22 us: shards(): lax.all_to_all(lax.all_to_all(spectra, 'lat', split_axis=0, concat_axis=3...]
  transfers between devices with their start and end apart: 7 -> 0, of which waited for: 4 -> 0; matrix products, arithmetic and copies ran while one was open for 7% -> 0% of each run, Pallas kernels for 0% -> 0%
where the time goes in v1:
time: 127 us
  Pallas kernels  123 us (97%)
  local copies, waits for them, and re-layouts  3.13 us (2%)
    pallas_call x1, Pallas kernels, shards(): pl.pallas_call(layer, out_shape=jax.ShapeDtypeStruct((ROWS, COLS, CH), BF...  123 us

profile of v1, /device:TPU:1, one launch (start us, length us, event | category | flops | bytes accessed | tf_op | source)
XLA Modules:
  0.0 127.0 jit_solution(15526973875262324256)
XLA Ops:
  0.0 0.8 reshape.6
  0.8 0.1 reshape.7
  0.9 0.6 pad_add_fusion.keys
  1.5 123.2 %layer.1 = bf16[8,256,256]{2,1,0:T(8,128)(2,1)} custom-call(bf16[8,256,256]{2,1,0:T(8,128)(2,1)} %field.1, s32[8,25]{1,0:T(8,128)} %basis.1, bf16[8,25]{1,0:T(8,128)(2,1)} %quad.1, bf16[4,2,128,128]{3,2,1,0:T(8,128)(2,1)} %mix_w.1, s32[8,128]{1,0:T(8,128)} %pad_add_fusion.keys, s32[512]{0:T(512)} %modes.1, bf16[2,512,512]{2,1,0:T(8,128)(2,1)} %legendre.1, ...), custom_call_target="tpu_custom_call" | custom-call | tf_op jit(solution)/shard_map/layer/pallas_call | solution.py:460
  124.7 2.3 %copy.14 = bf16[8,256,256]{2,1,0:T(8,128)(2,1)} copy(bf16[8,256,256]{2,1,0:T(8,128)(2,1)} %layer.1) | data formatting | bytes 2097152
  (1 shorter events, 0.0 us)

commit v2 on v1

v2 whole, which is shorter than its diff:
```python
import math

import jax
import jax.numpy as jnp
import numpy as np
from jax import lax
from jax.experimental import pallas as pl
from jax.experimental.pallas import tpu as pltpu
from jax.sharding import PartitionSpec as P

MESH = pl.DeviceIdType.MESH
BF = jnp.bfloat16
F32 = jnp.float32
I32 = jnp.int32

LATS = 64
LONS = 4
NLON = 1024
MODES = 512
ROWS = 8
COLS = 256
CH = 256
HALF = 128
WIN = 96
TILE = 64
RIM = 16


def wave_tables():
    q = (np.arange(MODES)[:, None] * np.arange(NLON)[None, :]) % NLON
    phase = 2.0 * np.pi * q / NLON
    waves = np.stack([np.cos(phase), -np.sin(phase)]) / math.sqrt(NLON)
    return waves


def dot(a, b):
    return jnp.dot(a, b, preferred_element_type=F32)


def gelu(x):
    return jax.nn.gelu(x, approximate=True)


def rows_of(start, size):
    return pl.ds(pl.multiple_of(start, 16), size)


def half_of(index):
    return pl.ds(pl.multiple_of(index * HALF, HALF), HALF)


def wrap(value, size):
    value = jnp.where(value >= size, value - size, value)
    return jnp.where(value < 0, value + size, value)


def one_hot(mask):
    return mask.astype(F32).astype(BF)


def iota(shape, dim):
    return lax.broadcasted_iota(I32, shape, dim)


def layer(
    field, basis, quad, mix_w, order, modes, legendre, filt, inner, outer, waves, waves_t,
    out,
    ext, wdisco, tab, tab_t, wav, wav_t, band, diag, sel, dsend, full, ssend, srecv, spec, leg, leg_t,
    fmat, ssend2, srecv2, zed, psend, precv, perm_a, perm_at, perm_b, perm_bt, w_in, w_out, w_filt, rows,
    load_sem, halo_send, halo_recv, d_send, d_recv, s_send, s_recv, b_send, b_recv, p_send, p_recv, o_sem,
):
    lat = lax.axis_index("lat")
    lon = lax.axis_index("lon")
    lat_x = lat // 32
    lat_z = (lat // 4) % 8
    lat_y = lat % 4
    my_h = lon // 2
    my_g = lon % 2
    north = wrap(lat - 1, LATS)
    south = wrap(lat + 1, LATS)
    west = wrap(lon - 1, LONS)
    east = wrap(lon + 1, LONS)
    my_pos = lat_y * 64 + (lat_x * 8 + lat_z) * 4 + lon
    my_src = lat * 2 + my_h

    barrier = pltpu.get_barrier_semaphore()

    def greet(to_lat, to_lon):
        pl.semaphore_signal(barrier, inc=1, device_id=(to_lat, to_lon), device_id_type=MESH)

    def greet_pair(n, carry):
        for to in (wrap(lat + n, LATS), wrap(lat - n, LATS)):
            for to_lon in range(LONS):
                greet(to, to_lon)
        return carry

    for n in range(1, LONS):
        greet(lat, wrap(lon + n, LONS))
    lax.fori_loop(1, LATS // 2, greet_pair, 0)
    for to_lon in range(LONS):
        greet(wrap(lat + LATS // 2, LATS), to_lon)

    loads = [
        pltpu.make_async_copy(field, ext.at[2 : 2 + ROWS, RIM : RIM + COLS, :], load_sem.at[0]),
        pltpu.make_async_copy(waves, wav, load_sem.at[1]),
        pltpu.make_async_copy(waves_t, wav_t, load_sem.at[2]),
        pltpu.make_async_copy(legendre, leg, load_sem.at[3]),
        pltpu.make_async_copy(inner, w_in, load_sem.at[4]),
        pltpu.make_async_copy(outer, w_out, load_sem.at[5]),
        pltpu.make_async_copy(filt, w_filt, load_sem.at[6]),
    ]
    for load in loads:
        load.start()
    for g in range(2):
        for k in range(4):
            pltpu.make_async_copy(
                mix_w.at[k, g], wdisco.at[g, k * HALF : (k + 1) * HALF, :], load_sem.at[7]
            ).start()

    point = iota((25, 512), 0)
    lane25 = iota((25, 512), 1)
    lane8 = iota((8, 512), 1)
    lat_row = lat * ROWS + iota((8, 512), 0) + lane8 // WIN - 2
    inside = (lat_row >= 0) & (lat_row < LATS * ROWS) & (lane8 < 5 * WIN)
    quads = quad[...]
    bases = basis[...].astype(F32).astype(BF)
    for dx in range(5):
        pick = one_hot(point == 5 * (lane25 // WIN) + dx)
        weight = jnp.where(inside, dot(quads, pick), 0.0)
        kind = dot(bases, pick)
        for k in range(4):
            sel[5 * k + dx] = jnp.where(kind == float(k), weight, 0.0)
    lane64 = iota((TILE, 512), 1)
    diag[...] = jnp.where(
        lane64 < 5 * WIN, lane64 % WIN - (RIM - 2) - iota((TILE, 512), 0), -1000
    )

    def band_row(a, carry):
        for piece in range(TILE // 16):
            at = slice(piece * 16, (piece + 1) * 16)
            hits = [diag[at, :] == dx for dx in range(5)]
            for k in range(4):
                values = jnp.zeros((16, 512), F32)
                for dx in range(5):
                    values = jnp.where(hits[dx], sel[5 * k + dx, pl.ds(a, 1), :], values)
                band[a, k * TILE + piece * 16 : k * TILE + (piece + 1) * 16, :] = values.astype(BF)
        return carry

    lax.fori_loop(0, 8, band_row, 0)

    row = iota((256, 256), 0)
    col = iota((256, 256), 1)

    def sent(n):
        return ((n // 4) % 2) * 128 + (n % 2) * 64 + (n // 8) * 2 + (n // 2) % 2

    def gathered(n):
        at = n % 8
        edge = jnp.where((at // 2 == 0) | (at // 2 == 3), 128, 0)
        src = ((n % 64) // 8) * 2 + at // 4
        return edge + src * 8 + (at % 2) * 4 + (n // 128) * 2 + (n // 64) % 2

    perm_a[...] = one_hot(col == sent(row))
    perm_at[...] = one_hot(row == sent(col))
    perm_b[...] = one_hot(col == gathered(row))
    perm_bt[...] = one_hot(row == gathered(col))

    natural = jnp.concatenate([order[...].astype(F32), jnp.zeros((4, HALF), F32)], axis=0)
    high = jnp.floor(natural * 0.5)
    lane_to = iota((HALF, 512), 1)
    stripe = one_hot(
        iota((HALF, 512), 0)
        == ((lane_to % HALF) // 8 % 4) * 32 + (lane_to // HALF) * 8 + lane_to % 8
    )
    spread = 2.0 * dot(high.astype(BF), stripe) + dot((natural - 2.0 * high).astype(BF), stripe)
    from_row = iota((8, 512), 0) == (iota((8, 512), 1) % HALF) // 32
    keys = jnp.sum(jnp.where(from_row, spread, 0.0), axis=0, keepdims=True)
    key_rows = [keys[:, y * HALF : (y + 1) * HALF] for y in range(4)]
    key_cols = jnp.transpose(
        jnp.concatenate(key_rows + [jnp.zeros((HALF - 4, HALF), F32)], axis=0)
    ).astype(I32)

    pl.semaphore_wait(barrier, LATS * LONS - 1)

    top, bottom = slice(0, 2), slice(ROWS - 2, ROWS)
    left, right = slice(0, RIM), slice(COLS - RIM, COLS)
    here_rows, here_cols = slice(2, 2 + ROWS), slice(RIM, RIM + COLS)
    above, below = slice(0, 2), slice(ROWS + 2, ROWS + 4)
    before, after = slice(0, RIM), slice(RIM + COLS, 2 * RIM + COLS)
    whole = slice(None)
    plan = [
        ((lat, east), (whole, right), (here_rows, before)),
        ((lat, west), (whole, left), (here_rows, after)),
        ((south, lon), (bottom, whole), (above, here_cols)),
        ((north, lon), (top, whole), (below, here_cols)),
        ((south, east), (bottom, right), (above, before)),
        ((south, west), (bottom, left), (above, after)),
        ((north, east), (top, right), (below, before)),
        ((north, west), (top, left), (below, after)),
    ]
    rims = []
    for n, (peer, (sr, sc), (dr, dc)) in enumerate(plan):
        rims.append(
            pltpu.make_async_remote_copy(
                field.at[sr, sc, :], ext.at[dr, dc, :], halo_send.at[n], halo_recv.at[n],
                device_id=peer, device_id_type=MESH,
            )
        )
    for rim in rims:
        rim.start()

    loads[1].wait()
    for y in range(4):
        hot = one_hot(iota((HALF, MODES), 1) == key_cols[:, y : y + 1])
        for r in range(2):
            tab[(2 * y + r) * HALF : (2 * y + r + 1) * HALF, :] = dot(hot, wav[r]).astype(BF)

    def conv_row(chunk, n):
        a = n + 2 if chunk == 0 else n + 4 * (n // 2)
        weights = band[a]
        parts = [[], []]
        for tile in range(COLS // TILE):
            j = tile * TILE
            window = jnp.concatenate(
                [ext[a + dy, j : j + WIN, :] for dy in range(5)] + [ext[a + 2, j : j + 32, :]],
                axis=0,
            )
            response = dot(weights, window).astype(BF)
            for g in range(2):
                parts[g].append(
                    jnp.concatenate(
                        [
                            response[k * TILE : (k + 1) * TILE, g * HALF : (g + 1) * HALF]
                            for k in range(4)
                        ],
                        axis=1,
                    )
                )
        for g in range(2):
            mixed = dot(jnp.concatenate(parts[g], axis=0), wdisco[g]).astype(BF)
            dsend[chunk * 4 + (n // 2) * 2 + g, :, half_of(n % 2)] = mixed

    def conv(chunk):
        def body(n, carry):
            conv_row(chunk, n)
            return carry

        lax.fori_loop(0, 4, body, 0)

    far = [(1 - my_h) * 2 + my_g, (1 - my_h) * 2 + 1 - my_g, my_h * 2 + 1 - my_g]
    my_cols = rows_of(lon * COLS, COLS)

    def d_start(chunk):
        for to in far:
            pltpu.make_async_remote_copy(
                dsend.at[chunk * 4 + to], full.at[chunk, my_cols, :], d_send, d_recv.at[chunk],
                device_id=(lat, to), device_id_type=MESH,
            ).start()
        pltpu.make_async_copy(
            dsend.at[chunk * 4 + lon], full.at[chunk, my_cols, :], d_recv.at[chunk]
        ).start()

    loads[0].wait()
    pltpu.make_async_copy(wdisco, wdisco, load_sem.at[7]).wait()
    rims[0].wait()
    rims[1].wait()
    conv(0)
    d_start(0)
    for rim in rims[2:]:
        rim.wait()
    conv(1)
    d_start(1)

    def s_send_all(chunk):
        def step(i, carry):
            y = wrap(lat_y + i, 4)
            waved = dot(tab[rows_of(y * 256, 256), :], full[chunk]).astype(BF)
            for q in range(2):
                stacked = jnp.concatenate(
                    [
                        waved[r * HALF + q * 64 : r * HALF + q * 64 + 64, a * HALF : (a + 1) * HALF]
                        for a in range(2)
                        for r in range(2)
                    ],
                    axis=0,
                )
                block = dot(perm_a[...], stacked).reshape(32, 8, HALF).astype(BF)
                ssend[pl.ds(chunk * 256 + y * 64 + q * 32, 32)] = block

            def source(x, z, to_lon):
                return ssend.at[chunk * 256 + y * 64 + (x * 8 + z) * 4 + to_lon]

            target = srecv.at[chunk * 128 + my_src, :, half_of(my_g)]
            for dz in (4, 3, -3, 2, -2, 1, -1, 0):
                z = wrap(lat_z + dz, 8)
                for dx in (1, 0):
                    x = wrap(lat_x + dx, 2)
                    for dl in (2, 3, 1, 0):
                        to_lon = wrap(lon + dl, LONS)

                        def remote():
                            pltpu.make_async_remote_copy(
                                source(x, z, to_lon), target, s_send, s_recv.at[chunk],
                                device_id=(x * 32 + z * 4 + y, to_lon), device_id_type=MESH,
                            ).start()

                        if dz == 0 and dx == 0 and dl == 0:
                            pl.when(i != 0)(remote)

                            @pl.when(i == 0)
                            def _():
                                pltpu.make_async_copy(
                                    source(x, z, to_lon), target, s_recv.at[chunk]
                                ).start()
                        else:
                            remote()
            return carry

        lax.fori_loop(0, 4, step, 0)

    loads[3].wait()
    for t in range(2):
        least = modes[(lat * LONS + lon) * 2 + t]
        masked = jnp.where(iota((MODES, MODES), 0) >= least, leg[t].astype(F32), 0.0)
        leg[t] = masked.astype(BF)
        leg_t[t] = jnp.transpose(masked).astype(BF)
    loads[6].wait()
    fmat[0:CH, 0:CH] = w_filt[0]
    fmat[0:CH, CH : 2 * CH] = w_filt[1]
    fmat[CH : 2 * CH, 0:CH] = -w_filt[1]
    fmat[CH : 2 * CH, CH : 2 * CH] = w_filt[0]

    for chunk in range(2):
        pltpu.make_async_copy(full.at[chunk], full.at[chunk], d_recv.at[chunk]).wait()
        s_send_all(chunk)

    loads[2].wait()
    for y in range(4):
        hot = one_hot(iota((MODES, HALF), 0) == key_rows[y].astype(I32))
        for r in range(2):
            tab_t[:, (2 * y + r) * HALF : (2 * y + r + 1) * HALF] = dot(wav_t[r], hot).astype(BF)

    for chunk in range(2):
        arrived = srecv.at[chunk * 128 : (chunk + 1) * 128]
        pltpu.make_async_copy(arrived, arrived, s_recv.at[chunk]).wait()

    def flat(block):
        return block.astype(F32).reshape(block.shape[0] * 8, block.shape[2]).astype(BF)

    for b in range(8):
        pair = [flat(srecv[chunk * 128 + b * 16 : chunk * 128 + (b + 1) * 16]) for chunk in range(2)]
        turned = dot(perm_b[...], jnp.concatenate(pair, axis=0)).astype(BF)
        for t in range(2):
            for r in range(2):
                spec[t, b * 64 : (b + 1) * 64, r * CH : (r + 1) * CH] = turned[
                    t * 128 + r * 64 : t * 128 + r * 64 + 64, :
                ]

    for t in range(2):
        coeffs = dot(leg[t], spec[t]).astype(BF)
        filtered = dot(coeffs, fmat[...]).astype(BF)
        back = dot(leg_t[t], filtered)
        scale = jnp.where(modes[(lat * LONS + lon) * 2 + t] == 0, 1.0, 2.0).astype(F32)
        spec[t] = (back * scale).astype(BF)

    for b in range(8):
        stacked = jnp.concatenate(
            [
                spec[t, b * 64 : (b + 1) * 64, r * CH : (r + 1) * CH]
                for t in range(2)
                for r in range(2)
            ],
            axis=0,
        )
        turned = dot(perm_bt[...], stacked)
        for chunk in range(2):
            ssend2[chunk * 128 + b * 16 : chunk * 128 + (b + 1) * 16] = (
                turned[chunk * 128 : (chunk + 1) * 128].reshape(16, 8, CH).astype(BF)
            )

    for chunk in range(2):

        def b_step(i, carry):
            y = wrap(lat_y + i, 4)
            target = srecv2.at[chunk * 256 + my_pos]
            for dz in (4, 3, -3, 2, -2, 1, -1, 0):
                z = wrap(lat_z + dz, 8)
                for dx in (1, 0):
                    x = wrap(lat_x + dx, 2)
                    to_lat = x * 32 + z * 4 + y
                    for to_lon in range(LONS):
                        source = ssend2.at[
                            chunk * 128 + to_lat * 2 + to_lon // 2,
                            :,
                            (to_lon % 2) * HALF : (to_lon % 2 + 1) * HALF,
                        ]

                        def remote():
                            pltpu.make_async_remote_copy(
                                source, target, b_send, b_recv.at[chunk],
                                device_id=(to_lat, to_lon), device_id_type=MESH,
                            ).start()

                        if dz == 0 and dx == 0:
                            own = (i == 0) & (lon == to_lon)
                            pl.when(jnp.logical_not(own))(remote)

                            @pl.when(own)
                            def _():
                                pltpu.make_async_copy(source, target, b_recv.at[chunk]).start()
                        else:
                            remote()
            return carry

        lax.fori_loop(0, 4, b_step, 0)

    loads[4].wait()
    loads[5].wait()

    for chunk in range(2):
        arrived = srecv2.at[chunk * 256 : (chunk + 1) * 256]
        pltpu.make_async_copy(arrived, arrived, b_recv.at[chunk]).wait()
        for q in range(8):
            start = chunk * 256 + q * 32
            turned = dot(perm_at[...], flat(srecv2[start : start + 32])).astype(BF)
            for a in range(2):
                for r in range(2):
                    put = (q // 2) * 256 + r * HALF + (q % 2) * 64
                    zed[chunk, put : put + 64, a * HALF : (a + 1) * HALF] = turned[
                        a * 128 + r * 64 : a * 128 + r * 64 + 64, :
                    ]
        for to in far + [lon]:
            part = rows_of(to * COLS, COLS)
            psend[chunk, part, :] = dot(tab_t[part, :], zed[chunk]).astype(BF)
            target = precv.at[chunk * 4 + lon]
            arrival = p_recv.at[chunk * 2 + my_h]
            if to is lon:
                pltpu.make_async_copy(psend.at[chunk, part, :], target, arrival).start()
            else:
                pltpu.make_async_remote_copy(
                    psend.at[chunk, part, :], target, p_send, arrival,
                    device_id=(lat, to), device_id_type=MESH,
                ).start()

    for chunk in range(2):
        for h in (my_h, 1 - my_h):
            arrived = precv.at[pl.ds(chunk * 4 + 2 * h, 2)]
            pltpu.make_async_copy(arrived, arrived, p_recv.at[chunk * 2 + h]).wait()

            def mlp_row(n, carry, h=h):
                lanes = half_of(n)
                first = chunk * 4 + 2 * h
                mixed = jnp.concatenate(
                    [
                        gelu(
                            precv[first + g, :, lanes].astype(F32)
                            + dsend[first + g, :, lanes].astype(F32)
                        )
                        for g in range(2)
                    ],
                    axis=1,
                ).astype(BF)
                hidden = gelu(dot(mixed, w_in[...])).astype(BF)
                a = 2 + 2 * h + n if chunk == 0 else 6 * h + n
                result = ext[a + 2, RIM : RIM + COLS, :].astype(F32) + dot(hidden, w_out[...])
                rows[a] = result.astype(BF)
                pltpu.make_async_copy(rows.at[a], out.at[a], o_sem).start()
                return carry

            lax.fori_loop(0, 2, mlp_row, 0)

    pltpu.make_async_copy(dsend.at[0:6], dsend.at[0:6], d_send).wait()
    pltpu.make_async_copy(ssend.at[0:510], ssend.at[0:510], s_send).wait()
    pltpu.make_async_copy(srecv2.at[0:510], srecv2.at[0:510], b_send).wait()
    pltpu.make_async_copy(precv.at[0:6], precv.at[0:6], p_send).wait()
    pltpu.make_async_copy(rows, rows, o_sem).wait()


def shards(
    grid_field, basis_index, quad_weight, disco_weight, mode_order, legendre, filter_weight,
    inner_weight, outer_weight,
):
    table = wave_tables()
    waves = jnp.asarray(table, BF)
    waves_t = jnp.asarray(np.swapaxes(table, 1, 2), BF)
    vmem = pl.BlockSpec(memory_space=pltpu.VMEM)
    smem = pl.BlockSpec(memory_space=pltpu.SMEM)
    anywhere = pl.BlockSpec(memory_space=pl.ANY)
    dma = pltpu.SemaphoreType.DMA
    scratch = [
        pltpu.VMEM((ROWS + 4, COLS + 2 * RIM, CH), BF),
        pltpu.VMEM((2, 512, HALF), BF),
        pltpu.VMEM((1024, NLON), BF),
        pltpu.VMEM((NLON, 1024), BF),
        pltpu.VMEM((2, MODES, NLON), BF),
        pltpu.VMEM((2, NLON, MODES), BF),
        pltpu.VMEM((ROWS, 4 * TILE, 512), BF),
        pltpu.VMEM((TILE, 512), I32),
        pltpu.VMEM((20, 8, 512), F32),
        pltpu.VMEM((8, COLS, CH), BF),
        pltpu.VMEM((2, NLON, CH), BF),
        pltpu.VMEM((512, 8, HALF), BF),
        pltpu.VMEM((256, 8, CH), BF),
        pltpu.VMEM((2, 512, 512), BF),
        pltpu.VMEM((2, 512, 512), BF),
        pltpu.VMEM((2, 512, 512), BF),
        pltpu.VMEM((512, 512), BF),
        pltpu.VMEM((256, 8, CH), BF),
        pltpu.VMEM((512, 8, HALF), BF),
        pltpu.VMEM((2, 1024, CH), BF),
        pltpu.VMEM((2, NLON, CH), BF),
        pltpu.VMEM((8, COLS, CH), BF),
        pltpu.VMEM((256, 256), BF),
        pltpu.VMEM((256, 256), BF),
        pltpu.VMEM((256, 256), BF),
        pltpu.VMEM((256, 256), BF),
        pltpu.VMEM((CH, 512), BF),
        pltpu.VMEM((512, CH), BF),
        pltpu.VMEM((2, CH, CH), BF),
        pltpu.VMEM((ROWS, COLS, CH), BF),
        dma((8,)),
        dma((8,)),
        dma((8,)),
        dma,
        dma((2,)),
        dma,
        dma((2,)),
        dma,
        dma((2,)),
        dma,
        dma((4,)),
        dma,
    ]
    return pl.pallas_call(
        layer,
        out_shape=jax.ShapeDtypeStruct((ROWS, COLS, CH), BF),
        in_specs=[
            anywhere, vmem, vmem, anywhere, vmem, smem, anywhere, anywhere, anywhere, anywhere,
            anywhere, anywhere,
        ],
        out_specs=anywhere,
        scratch_shapes=scratch,
        compiler_params=pltpu.CompilerParams(
            collective_id=0, has_side_effects=True, vmem_limit_bytes=56 * 1024 * 1024
        ),
        name="layer",
    )(
        grid_field, basis_index, quad_weight, disco_weight, mode_order.reshape(4, HALF), mode_order,
        legendre, filter_weight, inner_weight, outer_weight, waves, waves_t,
    )


def solution(mesh):
    in_specs = (
        P("lat", "lon", None),
        P("lat", None),
        P("lat", None),
        P(),
        P(),
        P(("lat", "lon"), None, None),
        P(),
        P(),
        P(),
    )
    out_specs = P("lat", "lon", None)
    return jax.shard_map(shards, mesh=mesh, in_specs=in_specs, out_specs=out_specs, check_vma=False)
```

time: 127 us -> 103 us (0.81)
  Pallas kernels: 123 us -> 100 us
    pallas_call x1, Pallas kernels: 123 us -> 100 us  [shards(): pl.pallas_call(layer, out_shape=jax.ShapeDtypeStruct((ROWS, COLS, CH), BF...]
where the time goes in v2:
time: 103 us
  Pallas kernels  100 us (97%)
  local copies, waits for them, and re-layouts  2.26 us (2%)
    pallas_call x1, Pallas kernels, shards(): pl.pallas_call(layer, out_shape=jax.ShapeDtypeStruct((ROWS, COLS, CH), BF...  100 us
    unnamed x1, local copies, waits for them, and re-layouts  2.26 us

profile of v2, /device:TPU:1, one launch (start us, length us, event | category | flops | bytes accessed | tf_op | source)
XLA Modules:
  0.0 102.6 jit_solution(13662949060204880341)
XLA Ops:
  0.0 100.3 %layer.1 = bf16[8,256,256]{2,1,0:T(8,128)(2,1)} custom-call(bf16[8,256,256]{2,1,0:T(8,128)(2,1)} %field.1, s32[8,25]{1,0:T(8,128)} %basis.1, bf16[8,25]{1,0:T(8,128)(2,1)} %quad.1, bf16[4,2,128,128]{3,2,1,0:T(8,128)(2,1)} %mix_w.1, s32[4,128]{1,0:T(4,128)} %bitcast.1, s32[512]{0:T(512)} %modes.1, bf16[2,512,512]{2,1,0:T(8,128)(2,1)} %legendre.1, ...), custom_call_target="tpu_custom_call" | custom-call | tf_op jit(solution)/shard_map/layer/pallas_call | solution.py:534
  100.3 2.3 %copy.13 = bf16[8,256,256]{2,1,0:T(8,128)(2,1)} copy(bf16[8,256,256]{2,1,0:T(8,128)(2,1)} %layer.1) | data formatting | bytes 2097152

commit v3 on v2

v3 whole, which is shorter than its diff:
```python
import math

import jax
import jax.numpy as jnp
import numpy as np
from jax import lax
from jax.experimental import pallas as pl
from jax.experimental.pallas import tpu as pltpu
from jax.sharding import PartitionSpec as P

MESH = pl.DeviceIdType.MESH
BF = jnp.bfloat16
F32 = jnp.float32
I32 = jnp.int32

LATS = 64
LONS = 4
NLON = 1024
MODES = 512
ROWS = 8
COLS = 256
CH = 256
HALF = 128
WIN = 96
TILE = 64
RIM = 16


def wave_tables():
    q = (np.arange(MODES)[:, None] * np.arange(NLON)[None, :]) % NLON
    phase = 2.0 * np.pi * q / NLON
    waves = np.stack([np.cos(phase), -np.sin(phase)]) / math.sqrt(NLON)
    return waves


def dot(a, b):
    return jnp.dot(a, b, preferred_element_type=F32)


def gelu(x):
    return jax.nn.gelu(x, approximate=True)


def rows_of(start, size):
    return pl.ds(pl.multiple_of(start, 16), size)


def half_of(index):
    return pl.ds(pl.multiple_of(index * HALF, HALF), HALF)


def wrap(value, size):
    value = jnp.where(value >= size, value - size, value)
    return jnp.where(value < 0, value + size, value)


def one_hot(mask):
    return mask.astype(F32).astype(BF)


def iota(shape, dim):
    return lax.broadcasted_iota(I32, shape, dim)


def layer(
    field, basis, quad, mix_w, order, modes, legendre, filt, inner, outer, waves, waves_t,
    out,
    ext, wdisco, tab, tab_t, wav, wav_t, band, diag, sel, dsend, full, ssend, srecv, spec, leg, leg_t,
    fmat, ssend2, srecv2, zed, acc, psend, precv, perm_a, perm_at, perm_b, perm_bt, w_in, w_out, w_filt, rows, relay,
    load_sem, halo_send, halo_recv, relay_sem, d_send, d_recv, s_send, s_recv, b_send, b_recv, p_send, p_recv, o_sem,
):
    lat = lax.axis_index("lat")
    lon = lax.axis_index("lon")
    lat_x = lat // 32
    lat_z = (lat // 4) % 8
    lat_y = lat % 4
    my_h = lon // 2
    my_g = lon % 2
    north = wrap(lat - 1, LATS)
    south = wrap(lat + 1, LATS)
    west = wrap(lon - 1, LONS)
    east = wrap(lon + 1, LONS)
    my_pos = lat_y * 64 + (lat_x * 8 + lat_z) * 4 + lon
    my_src = lat * 2 + my_h

    barrier = pltpu.get_barrier_semaphore()

    def greet(to_lat, to_lon):
        pl.semaphore_signal(barrier, inc=1, device_id=(to_lat, to_lon), device_id_type=MESH)

    def greet_pair(n, carry):
        for to in (wrap(lat + n, LATS), wrap(lat - n, LATS)):
            for to_lon in range(LONS):
                greet(to, to_lon)
        return carry

    for n in range(1, LONS):
        greet(lat, wrap(lon + n, LONS))
    lax.fori_loop(1, LATS // 2, greet_pair, 0)
    for to_lon in range(LONS):
        greet(wrap(lat + LATS // 2, LATS), to_lon)

    loads = [
        pltpu.make_async_copy(field, ext.at[2 : 2 + ROWS, RIM : RIM + COLS, :], load_sem.at[0]),
        pltpu.make_async_copy(waves, wav, load_sem.at[1]),
        pltpu.make_async_copy(waves_t, wav_t, load_sem.at[2]),
        pltpu.make_async_copy(legendre, leg, load_sem.at[3]),
        pltpu.make_async_copy(inner, w_in, load_sem.at[4]),
        pltpu.make_async_copy(outer, w_out, load_sem.at[5]),
        pltpu.make_async_copy(filt, w_filt, load_sem.at[6]),
    ]
    for load in loads:
        load.start()
    for g in range(2):
        for k in range(4):
            pltpu.make_async_copy(
                mix_w.at[k, g], wdisco.at[g, k * HALF : (k + 1) * HALF, :], load_sem.at[7]
            ).start()

    point = iota((25, 512), 0)
    lane25 = iota((25, 512), 1)
    lane8 = iota((8, 512), 1)
    lat_row = lat * ROWS + iota((8, 512), 0) + lane8 // WIN - 2
    inside = (lat_row >= 0) & (lat_row < LATS * ROWS) & (lane8 < 5 * WIN)
    quads = quad[...]
    bases = basis[...].astype(F32).astype(BF)
    for dx in range(5):
        pick = one_hot(point == 5 * (lane25 // WIN) + dx)
        weight = jnp.where(inside, dot(quads, pick), 0.0)
        kind = dot(bases, pick)
        for k in range(4):
            sel[5 * k + dx] = jnp.where(kind == float(k), weight, 0.0)
    lane64 = iota((TILE, 512), 1)
    diag[...] = jnp.where(
        lane64 < 5 * WIN, lane64 % WIN - (RIM - 2) - iota((TILE, 512), 0), -1000
    )

    def band_row(a, carry):
        for piece in range(TILE // 16):
            at = slice(piece * 16, (piece + 1) * 16)
            hits = [diag[at, :] == dx for dx in range(5)]
            for k in range(4):
                values = jnp.zeros((16, 512), F32)
                for dx in range(5):
                    values = jnp.where(hits[dx], sel[5 * k + dx, pl.ds(a, 1), :], values)
                band[a, k * TILE + piece * 16 : k * TILE + (piece + 1) * 16, :] = values.astype(BF)
        return carry


    def edge_band(n, carry):
        return band_row(jnp.where(n < 2, n, n + 4), carry)

    lax.fori_loop(2, 6, band_row, 0)

    pl.semaphore_wait(barrier, LATS * LONS - 1)

    top, bottom = slice(0, 2), slice(ROWS - 2, ROWS)
    left, right = slice(0, RIM), slice(COLS - RIM, COLS)
    here_rows, here_cols = slice(2, 2 + ROWS), slice(RIM, RIM + COLS)
    above, below = slice(0, 2), slice(ROWS + 2, ROWS + 4)
    before, after = slice(0, RIM), slice(RIM + COLS, 2 * RIM + COLS)
    whole = slice(None)
    plan = [
        ((lat, east), (whole, right), (here_rows, before)),
        ((lat, west), (whole, left), (here_rows, after)),
        ((south, lon), (bottom, whole), (above, here_cols)),
        ((north, lon), (top, whole), (below, here_cols)),
        ((south, east), (bottom, right), (above, before)),
        ((south, west), (bottom, left), (above, after)),
        ((north, east), (top, right), (below, before)),
        ((north, west), (top, left), (below, after)),
    ]
    rims = []
    for n, (peer, (sr, sc), (dr, dc)) in enumerate(plan):
        rims.append(
            pltpu.make_async_remote_copy(
                field.at[sr, sc, :], ext.at[dr, dc, :], halo_send.at[n], halo_recv.at[n],
                device_id=peer, device_id_type=MESH,
            )
        )
    for rim in rims[:2]:
        rim.start()
    for n in (2, 4, 5):
        pl.when((lat != LATS - 1) if n > 2 else (lat != LATS - 1) & (lat != 31))(rims[n].start)
    for n in (3, 6, 7):
        pl.when((lat != 0) if n > 3 else (lat != 0) & (lat != 32))(rims[n].start)

    quarter = COLS // 4

    def pieces(n, source_rows, target_rows, direct, peer, first_relay):
        for p in range(4):
            cols = slice(p * quarter, (p + 1) * quarter)
            if p == direct:
                put = ext.at[target_rows, RIM + p * quarter : RIM + (p + 1) * quarter, :]
            pltpu.make_async_remote_copy(
                field.at[source_rows, cols, :],
                put if p == direct else relay,
                halo_send.at[n],
                halo_recv.at[n] if p == direct else relay_sem.at[0],
                device_id=(peer if p == direct else first_relay + p, lon), device_id_type=MESH,
            ).start()

    @pl.when(lat == 31)
    def _():
        pieces(2, bottom, above, 3, 32, 0)

    @pl.when(lat == 32)
    def _():
        pieces(3, top, below, 0, 31, 60)

    def forward(n, target_rows, p, peer):
        put = ext.at[target_rows, rows_of(RIM + p * quarter, quarter), :]
        pltpu.make_async_copy(relay, relay, relay_sem.at[0]).wait()
        pltpu.make_async_remote_copy(
            relay, put, relay_sem.at[1], halo_recv.at[n],
            device_id=(peer, lon), device_id_type=MESH,
        ).start()

    def forward_rows():
        pl.when(lat < 3)(lambda: forward(2, above, lat, 32))
        pl.when(lat > 60)(lambda: forward(3, below, lat - 60, 31))

    def wait_rows():
        for n in (2, 4, 5):
            pl.when(lat != LATS - 1)(rims[n].wait_send)
            pl.when(lat != 0)(rims[n].wait_recv)
        for n in (3, 6, 7):
            pl.when(lat != 0)(rims[n].wait_send)
            pl.when(lat != LATS - 1)(rims[n].wait_recv)

    @pl.when(lat == 0)
    def _():
        ext[above] = jnp.zeros((2, COLS + 2 * RIM, CH), BF)

    @pl.when(lat == LATS - 1)
    def _():
        ext[below] = jnp.zeros((2, COLS + 2 * RIM, CH), BF)

    far_h = 1 - my_h
    my_cols = rows_of(lon * COLS, COLS)

    def row_of(c, h):
        return jnp.where(h == 0, 3 - c, 4 + c)

    def conv(c, tiles):
        done = []
        for h in (far_h, my_h):
            a = row_of(c, h)
            weights = band[a]
            parts = [[], []]
            for tile in tiles:
                j = tile * TILE
                window = jnp.concatenate(
                    [ext[a + dy, j : j + WIN, :] for dy in range(5)] + [ext[a + 2, j : j + 32, :]],
                    axis=0,
                )
                response = dot(weights, window).astype(BF)
                for g in range(2):
                    parts[g].append(
                        jnp.concatenate(
                            [
                                response[k * TILE : (k + 1) * TILE, g * HALF : (g + 1) * HALF]
                                for k in range(4)
                            ],
                            axis=1,
                        )
                    )
            done.append(parts)
        for h, parts in zip((far_h, my_h), done):
            for g in range(2):
                mixed = dot(jnp.concatenate(parts[g], axis=0), wdisco[g]).astype(BF)
                for n, tile in enumerate(tiles):
                    dsend[c * 4 + 2 * h + g, tile * TILE : (tile + 1) * TILE, :] = mixed[
                        n * TILE : (n + 1) * TILE, :
                    ]

    def d_start(c):
        target = full.at[my_cols, c * HALF : (c + 1) * HALF]
        for to in (far_h * 2 + my_g, far_h * 2 + 1 - my_g, my_h * 2 + 1 - my_g):
            pltpu.make_async_remote_copy(
                dsend.at[c * 4 + to], target, d_send, d_recv.at[c],
                device_id=(lat, to), device_id_type=MESH,
            ).start()
        pltpu.make_async_copy(dsend.at[c * 4 + lon], target, d_recv.at[c]).start()

    def d_wait(c):
        arrived = full.at[:, c * HALF : (c + 1) * HALF]
        pltpu.make_async_copy(arrived, arrived, d_recv.at[c]).wait()

    loads[0].wait()
    pltpu.make_async_copy(wdisco, wdisco, load_sem.at[7]).wait()
    conv(0, (1, 2))
    conv(1, (1, 2))

    row = iota((256, 256), 0)
    col = iota((256, 256), 1)

    def paired(n):
        return (n % 2) * 128 + n // 2

    def gathered(n):
        at = n % 8
        place = jnp.where(at < 4, 3 - at, at)
        return ((n % 128) // 8) * 16 + place * 2 + n // 128

    perm_a[...] = one_hot(col == paired(row))
    perm_at[...] = one_hot(row == paired(col))
    perm_b[...] = one_hot(col == gathered(row))
    perm_bt[...] = one_hot(row == gathered(col))

    natural = jnp.concatenate([order[...].astype(F32), jnp.zeros((4, HALF), F32)], axis=0)
    high = jnp.floor(natural * 0.5)
    lane_to = iota((HALF, 512), 1)
    stripe = one_hot(
        iota((HALF, 512), 0)
        == (lane_to // 4 % 4) * 32 + (lane_to // 64 % 4) * 8 + (lane_to % 4) * 2 + lane_to // 256
    )
    spread = 2.0 * dot(high.astype(BF), stripe) + dot((natural - 2.0 * high).astype(BF), stripe)
    from_row = iota((8, 512), 0) == iota((8, 512), 1) // 16 % 4
    keys = jnp.sum(jnp.where(from_row, spread, 0.0), axis=0, keepdims=True)
    key_rows = [keys[:, n * HALF : (n + 1) * HALF] for n in range(4)]
    key_cols = jnp.transpose(
        jnp.concatenate(key_rows + [jnp.zeros((HALF - 4, HALF), F32)], axis=0)
    ).astype(I32)

    lax.fori_loop(0, 4, edge_band, 0)
    rims[0].wait()
    rims[1].wait()
    conv(0, (0, 3))
    d_start(0)
    conv(1, (0, 3))
    d_start(1)

    loads[1].wait()
    for n in range(4):
        hot = one_hot(iota((HALF, MODES), 1) == key_cols[:, n : n + 1])
        both = jnp.concatenate([dot(hot, wav[r]).astype(BF) for r in range(2)], axis=0)
        tab[n * 256 : (n + 1) * 256, :] = dot(perm_a[...], both).astype(BF)

    def each_device(remote, local):
        def step(i, carry):
            y = wrap(lat_y + i, 4)
            for dz in (4, 3, -3, 2, -2, 1, -1, 0):
                z = wrap(lat_z + dz, 8)
                for dx in (1, 0):
                    x = wrap(lat_x + dx, 2)
                    xz = x * 8 + z
                    for h, g in ((far_h, my_g), (far_h, 1 - my_g), (my_h, 1 - my_g), (my_h, my_g)):
                        peer = (xz * 4 + y, h, g, y * 64 + xz * 4 + 2 * h + g)
                        if dz == 0 and dx == 0 and h is my_h and g is my_g:
                            pl.when(i != 0)(lambda: remote(*peer))
                            pl.when(i == 0)(lambda: local(*peer))
                        else:
                            remote(*peer)
            return carry

        lax.fori_loop(0, 4, step, 0)

    def s_send_blocks(t, first, last):
        target = srecv.at[t * 256 + my_g * 128 + my_src, first:last]
        arrival = s_recv.at[t]

        def remote(to_lat, h, g, pos):
            pltpu.make_async_remote_copy(
                ssend.at[t * 256 + pos, first:last], target, s_send, arrival,
                device_id=(to_lat, 2 * h + g), device_id_type=MESH,
            ).start()

        def local(to_lat, h, g, pos):
            pltpu.make_async_copy(ssend.at[t * 256 + pos, first:last], target, arrival).start()

        each_device(remote, local)

    def wave(t, first, last):
        waved = dot(tab[t * 512 : (t + 1) * 512, :], full[:, first * HALF : last * HALF])
        for c in range(first, last):
            at = (c - first) * HALF
            ssend[t * 256 : (t + 1) * 256, c] = (
                waved[:, at : at + HALF].reshape(256, 2, HALF).astype(BF)
            )

    forward_rows()
    wait_rows()
    for c in (2, 3):
        conv(c, (0, 1, 2, 3))
        d_start(c)
    d_wait(0)
    wave(0, 0, 1)
    s_send_blocks(0, 0, 1)
    d_wait(1)
    wave(0, 1, 2)
    s_send_blocks(0, 1, 2)

    loads[3].wait()
    for t in range(2):
        least = modes[(lat * LONS + lon) * 2 + t]
        masked = jnp.where(iota((MODES, MODES), 0) >= least, leg[t].astype(F32), 0.0)
        leg[t] = masked.astype(BF)
        leg_t[t] = jnp.transpose(masked).astype(BF)
    loads[6].wait()
    fmat[0:CH, 0:CH] = w_filt[0]
    fmat[0:CH, CH : 2 * CH] = w_filt[1]
    fmat[CH : 2 * CH, 0:CH] = -w_filt[1]
    fmat[CH : 2 * CH, CH : 2 * CH] = w_filt[0]

    d_wait(2)
    d_wait(3)
    wave(0, 2, 4)
    s_send_blocks(0, 2, 4)
    wave(1, 0, 4)
    s_send_blocks(1, 0, 4)

    loads[2].wait()
    for n in range(4):
        hot = one_hot(iota((MODES, HALF), 0) == key_rows[n].astype(I32))
        both = jnp.concatenate([dot(wav_t[r], hot).astype(BF) for r in range(2)], axis=1)
        tab_t[:, n * 256 : (n + 1) * 256] = dot(both, perm_at[...]).astype(BF)

    def b_send_blocks(t, first, last, arrival):
        target = srecv2.at[t * 256 + my_pos, first:last]

        def source(to_lat, h, g):
            return ssend2.at[t * 256 + g * 128 + to_lat * 2 + h, first:last]

        def remote(to_lat, h, g, pos):
            pltpu.make_async_remote_copy(
                source(to_lat, h, g), target, b_send, arrival,
                device_id=(to_lat, 2 * h + g), device_id_type=MESH,
            ).start()

        def local(to_lat, h, g, pos):
            pltpu.make_async_copy(source(to_lat, h, g), target, arrival).start()

        each_device(remote, local)

    cuts = ((0, 1), (1, 2), (2, 3), (3, 4))
    for t in range(2):
        arrived = srecv.at[t * 256 : (t + 1) * 256]
        pltpu.make_async_copy(arrived, arrived, s_recv.at[t]).wait()
        for b in range(4):
            sides = [
                srecv[t * 256 + g * 128 + b * 32 : t * 256 + g * 128 + (b + 1) * 32].reshape(
                    256, HALF
                )
                for g in range(2)
            ]
            turned = dot(perm_b[...], jnp.concatenate(sides, axis=1)).astype(BF)
            for r in range(2):
                spec[b * 128 : (b + 1) * 128, r * CH : (r + 1) * CH] = turned[
                    r * 128 : (r + 1) * 128, :
                ]
        coeffs = dot(leg[t], spec[...]).astype(BF)
        filtered = dot(coeffs, fmat[...]).astype(BF)
        back = dot(leg_t[t], filtered)
        scale = jnp.where(modes[(lat * LONS + lon) * 2 + t] == 0, 1.0, 2.0).astype(F32)
        spec[...] = (back * scale).astype(BF)
        for b in range(4):
            stacked = jnp.concatenate(
                [spec[b * 128 : (b + 1) * 128, r * CH : (r + 1) * CH] for r in range(2)], axis=0
            )
            turned = dot(perm_bt[...], stacked)
            for g in range(2):
                ssend2[t * 256 + g * 128 + b * 32 : t * 256 + g * 128 + (b + 1) * 32] = (
                    turned[:, g * HALF : (g + 1) * HALF].reshape(32, 4, 2, HALF).astype(BF)
                )
        if t == 0:
            b_send_blocks(0, 0, 4, b_recv.at[0])
        else:
            for n, (first, last) in enumerate(cuts):
                b_send_blocks(1, first, last, b_recv.at[1 + n])

    loads[4].wait()
    loads[5].wait()

    def unpack(t, first, last):
        for c in range(first, last):
            zed[t, :, c * HALF : (c + 1) * HALF] = srecv2[t * 256 : (t + 1) * 256, c].reshape(
                512, HALF
            )

    arrived = srecv2.at[0:256]
    pltpu.make_async_copy(arrived, arrived, b_recv.at[0]).wait()
    unpack(0, 0, 4)

    def first_half(n, carry):
        part = rows_of(n * 256, 256)
        acc[part, :] = dot(tab_t[part, 0:512], zed[0])
        return carry

    lax.fori_loop(0, 4, first_half, 0)

    near = my_h * 2 + 1 - my_g
    for n, (first, last) in enumerate(cuts):
        arrived = srecv2.at[256:512, first:last]
        pltpu.make_async_copy(arrived, arrived, b_recv.at[1 + n]).wait()
        unpack(1, first, last)
        for c in range(first, last):
            lanes = slice(c * HALF, (c + 1) * HALF)
            target = precv.at[c * 4 + lon]
            arrival = p_recv.at[c * 2 + my_h]
            for to in (far_h * 2 + my_g, far_h * 2 + 1 - my_g, near, lon):
                part = rows_of(to * COLS, COLS)
                total = acc[part, lanes] + dot(tab_t[part, 512:1024], zed[1, :, lanes])
                psend[c, part, :] = total.astype(BF)
                if to is lon:
                    pltpu.make_async_copy(psend.at[c, part, :], target, arrival).start()
                else:
                    pltpu.make_async_remote_copy(
                        psend.at[c, part, :], target, p_send, arrival,
                        device_id=(lat, to), device_id_type=MESH,
                    ).start()

    def mlp(c, carry):
        for h in (my_h, far_h):
            first = c * 4 + 2 * h
            arrived = precv.at[pl.ds(first, 2)]
            pltpu.make_async_copy(arrived, arrived, p_recv.at[c * 2 + h]).wait()
            mixed = jnp.concatenate(
                [
                    gelu(precv[first + g].astype(F32) + dsend[first + g].astype(F32))
                    for g in range(2)
                ],
                axis=1,
            ).astype(BF)
            hidden = gelu(dot(mixed, w_in[...])).astype(BF)
            a = row_of(c, h)
            result = ext[a + 2, RIM : RIM + COLS, :].astype(F32) + dot(hidden, w_out[...])
            rows[a] = result.astype(BF)
            pltpu.make_async_copy(rows.at[a], out.at[a], o_sem).start()
        return carry

    lax.fori_loop(0, 4, mlp, 0)

    @pl.when((lat < 3) | (lat > 60))
    def _():
        pltpu.make_async_copy(relay, relay, relay_sem.at[1]).wait()

    pltpu.make_async_copy(dsend.at[0:12], dsend.at[0:12], d_send).wait()
    pltpu.make_async_copy(ssend.at[0:510], ssend.at[0:510], s_send).wait()
    pltpu.make_async_copy(ssend2.at[0:510], ssend2.at[0:510], b_send).wait()
    pltpu.make_async_copy(precv.at[0:12], precv.at[0:12], p_send).wait()
    pltpu.make_async_copy(rows, rows, o_sem).wait()


def shards(
    grid_field, basis_index, quad_weight, disco_weight, mode_order, legendre, filter_weight,
    inner_weight, outer_weight,
):
    table = wave_tables()
    waves = jnp.asarray(table, BF)
    waves_t = jnp.asarray(np.swapaxes(table, 1, 2), BF)
    vmem = pl.BlockSpec(memory_space=pltpu.VMEM)
    smem = pl.BlockSpec(memory_space=pltpu.SMEM)
    anywhere = pl.BlockSpec(memory_space=pl.ANY)
    hbm = pl.BlockSpec(memory_space=pltpu.HBM)
    dma = pltpu.SemaphoreType.DMA
    scratch = [
        pltpu.VMEM((ROWS + 4, COLS + 2 * RIM, CH), BF),
        pltpu.VMEM((2, 512, HALF), BF),
        pltpu.VMEM((1024, NLON), BF),
        pltpu.VMEM((NLON, 1024), BF),
        pltpu.VMEM((2, MODES, NLON), BF),
        pltpu.VMEM((2, NLON, MODES), BF),
        pltpu.VMEM((ROWS, 4 * TILE, 512), BF),
        pltpu.VMEM((TILE, 512), I32),
        pltpu.VMEM((20, 8, 512), F32),
        pltpu.VMEM((16, COLS, HALF), BF),
        pltpu.VMEM((NLON, 512), BF),
        pltpu.VMEM((512, 4, 2, HALF), BF),
        pltpu.VMEM((512, 4, 2, HALF), BF),
        pltpu.VMEM((512, 512), BF),
        pltpu.VMEM((2, 512, 512), BF),
        pltpu.VMEM((2, 512, 512), BF),
        pltpu.VMEM((512, 512), BF),
        pltpu.VMEM((512, 4, 2, HALF), BF),
        pltpu.VMEM((512, 4, 2, HALF), BF),
        pltpu.VMEM((2, 512, 512), BF),
        pltpu.VMEM((NLON, 512), F32),
        pltpu.VMEM((4, NLON, HALF), BF),
        pltpu.VMEM((16, COLS, HALF), BF),
        pltpu.VMEM((256, 256), BF),
        pltpu.VMEM((256, 256), BF),
        pltpu.VMEM((256, 256), BF),
        pltpu.VMEM((256, 256), BF),
        pltpu.VMEM((CH, 512), BF),
        pltpu.VMEM((512, CH), BF),
        pltpu.VMEM((2, CH, CH), BF),
        pltpu.VMEM((ROWS, COLS, CH), BF),
        pltpu.VMEM((2, COLS // 4, CH), BF),
        dma((8,)),
        dma((8,)),
        dma((8,)),
        dma((2,)),
        dma,
        dma((4,)),
        dma,
        dma((2,)),
        dma,
        dma((5,)),
        dma,
        dma((8,)),
        dma,
    ]
    return pl.pallas_call(
        layer,
        out_shape=jax.ShapeDtypeStruct((ROWS, COLS, CH), BF),
        in_specs=[
            hbm, vmem, vmem, hbm, vmem, smem, hbm, hbm, hbm, hbm,
            hbm, hbm,
        ],
        out_specs=anywhere,
        scratch_shapes=scratch,
        compiler_params=pltpu.CompilerParams(
            collective_id=0, has_side_effects=True, vmem_limit_bytes=56 * 1024 * 1024
        ),
        name="layer",
    )(
        grid_field, basis_index, quad_weight, disco_weight, mode_order.reshape(4, HALF), mode_order,
        legendre, filter_weight, inner_weight, outer_weight, waves, waves_t,
    )


def solution(mesh):
    in_specs = (
        P("lat", "lon", None),
        P("lat", None),
        P("lat", None),
        P(),
        P(),
        P(("lat", "lon"), None, None),
        P(),
        P(),
        P(),
    )
    out_specs = P("lat", "lon", None)
    return jax.shard_map(shards, mesh=mesh, in_specs=in_specs, out_specs=out_specs, check_vma=False)
```

time: 103 us -> 93.5 us (0.908)
  Pallas kernels: 100 us -> 91.1 us
    pallas_call x1, Pallas kernels: 100 us -> 91.1 us  [shards(): pl.pallas_call(layer, out_shape=jax.ShapeDtypeStruct((ROWS, COLS, CH), BF...]
where the time goes in v3:
time: 93.5 us; the launch traced here: 93.4 us
  Pallas kernels  91.1 us (97%)
  local copies, waits for them, and re-layouts  2.26 us (2%)
    pallas_call x1, Pallas kernels, shards(): pl.pallas_call(layer, out_shape=jax.ShapeDtypeStruct((ROWS, COLS, CH), BF...  91.1 us
    unnamed x1, local copies, waits for them, and re-layouts  2.26 us

profile of v3, /device:TPU:1, one launch (start us, length us, event | category | flops | bytes accessed | tf_op | source)
XLA Modules:
  0.0 93.4 jit_solution(8906989318627425264)
XLA Ops:
  0.0 91.1 %layer.1 = bf16[8,256,256]{2,1,0:T(8,128)(2,1)} custom-call(bf16[8,256,256]{2,1,0:T(8,128)(2,1)} %field.1, s32[8,25]{1,0:T(8,128)} %basis.1, bf16[8,25]{1,0:T(8,128)(2,1)} %quad.1, bf16[4,2,128,128]{3,2,1,0:T(8,128)(2,1)} %mix_w.1, s32[4,128]{1,0:T(4,128)} %bitcast.1, s32[512]{0:T(512)} %modes.1, bf16[2,512,512]{2,1,0:T(8,128)(2,1)} %legendre.1, ...), custom_call_target="tpu_custom_call" | custom-call | tf_op jit(solution)/shard_map/layer/pallas_call | solution.py:604
  91.1 2.3 %copy.13 = bf16[8,256,256]{2,1,0:T(8,128)(2,1)} copy(bf16[8,256,256]{2,1,0:T(8,128)(2,1)} %layer.1) | data formatting | bytes 2097152

commit v4 on v3

--- a/solution.py
+++ b/solution.py
@@ -185,40 +185,39 @@
     for n in (3, 6, 7):
         pl.when((lat != 0) if n > 3 else (lat != 0) & (lat != 32))(rims[n].start)
 
-    quarter = COLS // 4
-
-    def pieces(n, source_rows, target_rows, direct, peer, first_relay):
-        for p in range(4):
-            cols = slice(p * quarter, (p + 1) * quarter)
-            if p == direct:
-                put = ext.at[target_rows, RIM + p * quarter : RIM + (p + 1) * quarter, :]
+    ways = ((0, HALF), (HALF, HALF))
+
+    def pieces(n, source_rows, target_rows, peer, relays):
+        for (start, width), to in zip(ways, (peer,) + relays):
+            put = ext.at[target_rows, RIM + start : RIM + start + width, :]
             pltpu.make_async_remote_copy(
-                field.at[source_rows, cols, :],
-                put if p == direct else relay,
+                field.at[source_rows, start : start + width, :],
+                put if to == peer else relay,
                 halo_send.at[n],
-                halo_recv.at[n] if p == direct else relay_sem.at[0],
-                device_id=(peer if p == direct else first_relay + p, lon), device_id_type=MESH,
+                halo_recv.at[n] if to == peer else relay_sem.at[0],
+                device_id=(to, lon), device_id_type=MESH,
             ).start()
 
     @pl.when(lat == 31)
     def _():
-        pieces(2, bottom, above, 3, 32, 0)
+        pieces(2, bottom, above, 32, (63,))
 
     @pl.when(lat == 32)
     def _():
-        pieces(3, top, below, 0, 31, 60)
-
-    def forward(n, target_rows, p, peer):
-        put = ext.at[target_rows, rows_of(RIM + p * quarter, quarter), :]
+        pieces(3, top, below, 31, (0,))
+
+    def forward(n, target_rows, way, peer):
+        start, width = ways[way]
         pltpu.make_async_copy(relay, relay, relay_sem.at[0]).wait()
         pltpu.make_async_remote_copy(
-            relay, put, relay_sem.at[1], halo_recv.at[n],
+            relay, ext.at[target_rows, RIM + start : RIM + start + width, :],
+            relay_sem.at[1], halo_recv.at[n],
             device_id=(peer, lon), device_id_type=MESH,
         ).start()
 
     def forward_rows():
-        pl.when(lat < 3)(lambda: forward(2, above, lat, 32))
-        pl.when(lat > 60)(lambda: forward(3, below, lat - 60, 31))
+        pl.when(lat == 63)(lambda: forward(2, above, 1, 32))
+        pl.when(lat == 0)(lambda: forward(3, below, 1, 31))
 
     def wait_rows():
         for n in (2, 4, 5):
@@ -330,6 +329,7 @@
     d_start(0)
     conv(1, (0, 3))
     d_start(1)
+    forward_rows()
 
     loads[1].wait()
     for n in range(4):
@@ -379,7 +379,6 @@
                 waved[:, at : at + HALF].reshape(256, 2, HALF).astype(BF)
             )
 
-    forward_rows()
     wait_rows()
     for c in (2, 3):
         conv(c, (0, 1, 2, 3))
@@ -433,7 +432,7 @@
 
         each_device(remote, local)
 
-    cuts = ((0, 1), (1, 2), (2, 3), (3, 4))
+    cuts = ((0, 1), (1, 2), (2, 4))
     for t in range(2):
         arrived = srecv.at[t * 256 : (t + 1) * 256]
         pltpu.make_async_copy(arrived, arrived, s_recv.at[t]).wait()
@@ -478,6 +477,8 @@
                 512, HALF
             )
 
+    near = my_h * 2 + 1 - my_g
+
     arrived = srecv2.at[0:256]
     pltpu.make_async_copy(arrived, arrived, b_recv.at[0]).wait()
     unpack(0, 0, 4)
@@ -489,29 +490,25 @@
 
     lax.fori_loop(0, 4, first_half, 0)
 
-    near = my_h * 2 + 1 - my_g
-    for n, (first, last) in enumerate(cuts):
-        arrived = srecv2.at[256:512, first:last]
-        pltpu.make_async_copy(arrived, arrived, b_recv.at[1 + n]).wait()
-        unpack(1, first, last)
-        for c in range(first, last):
-            lanes = slice(c * HALF, (c + 1) * HALF)
-            target = precv.at[c * 4 + lon]
-            arrival = p_recv.at[c * 2 + my_h]
-            for to in (far_h * 2 + my_g, far_h * 2 + 1 - my_g, near, lon):
-                part = rows_of(to * COLS, COLS)
-                total = acc[part, lanes] + dot(tab_t[part, 512:1024], zed[1, :, lanes])
-                psend[c, part, :] = total.astype(BF)
-                if to is lon:
-                    pltpu.make_async_copy(psend.at[c, part, :], target, arrival).start()
-                else:
-                    pltpu.make_async_remote_copy(
-                        psend.at[c, part, :], target, p_send, arrival,
-                        device_id=(lat, to), device_id_type=MESH,
-                    ).start()
-
-    def mlp(c, carry):
-        for h in (my_h, far_h):
+    def second_half(c):
+        lanes = slice(c * HALF, (c + 1) * HALF)
+        target = precv.at[c * 4 + lon]
+        arrival = p_recv.at[c * 2 + my_h]
+        for to in (far_h * 2 + my_g, far_h * 2 + 1 - my_g, near, lon):
+            part = rows_of(to * COLS, COLS)
+            total = acc[part, lanes] + dot(tab_t[part, 512:1024], zed[1, :, lanes])
+            psend[c, part, :] = total.astype(BF)
+            if to is lon:
+                pltpu.make_async_copy(psend.at[c, part, :], target, arrival).start()
+            else:
+                pltpu.make_async_remote_copy(
+                    psend.at[c, part, :], target, p_send, arrival,
+                    device_id=(lat, to), device_id_type=MESH,
+                ).start()
+
+    def mlp(c):
+        def one(n, carry):
+            h = jnp.where(n == 0, my_h, far_h)
             first = c * 4 + 2 * h
             arrived = precv.at[pl.ds(first, 2)]
             pltpu.make_async_copy(arrived, arrived, p_recv.at[c * 2 + h]).wait()
@@ -527,11 +524,20 @@
             result = ext[a + 2, RIM : RIM + COLS, :].astype(F32) + dot(hidden, w_out[...])
             rows[a] = result.astype(BF)
             pltpu.make_async_copy(rows.at[a], out.at[a], o_sem).start()
-        return carry
-
-    lax.fori_loop(0, 4, mlp, 0)
-
-    @pl.when((lat < 3) | (lat > 60))
+            return carry
+
+        lax.fori_loop(0, 2, one, 0)
+
+    for n, (first, last) in enumerate(cuts):
+        arrived = srecv2.at[256:512, first:last]
+        pltpu.make_async_copy(arrived, arrived, b_recv.at[1 + n]).wait()
+        for c in range(first, last):
+            unpack(1, c, c + 1)
+            second_half(c)
+    for c in range(4):
+        mlp(c)
+
+    @pl.when((lat == 0) | (lat == 63))
     def _():
         pltpu.make_async_copy(relay, relay, relay_sem.at[1]).wait()
 
@@ -586,7 +592,7 @@
         pltpu.VMEM((512, CH), BF),
         pltpu.VMEM((2, CH, CH), BF),
         pltpu.VMEM((ROWS, COLS, CH), BF),
-        pltpu.VMEM((2, COLS // 4, CH), BF),
+        pltpu.VMEM((2, HALF, CH), BF),
         dma((8,)),
         dma((8,)),
         dma((8,)),
@@ -596,14 +602,14 @@
         dma,
         dma((2,)),
         dma,
-        dma((5,)),
+        dma((4,)),
         dma,
         dma((8,)),
         dma,
     ]
     return pl.pallas_call(
         layer,
-        out_shape=jax.ShapeDtypeStruct((ROWS, COLS, CH), BF),
+        out_shape=pltpu.VMEM((ROWS, COLS, CH), BF),
         in_specs=[
             hbm, vmem, vmem, hbm, vmem, smem, hbm, hbm, hbm, hbm,
             hbm, hbm,

time: 93.5 us -> 91.3 us (0.976)
  local copies, waits for them, and re-layouts: 2.26 us -> 0.97 us
    unnamed x1, local copies, waits for them, and re-layouts: 2.26 us -> 0.97 us
where the time goes in v4:
time: 91.3 us; the launch traced here: 91.2 us
  Pallas kernels  90.2 us (99%)
  local copies, waits for them, and re-layouts  0.97 us (1%)
    pallas_call x1, Pallas kernels, shards(): pl.pallas_call(layer, out_shape=pltpu.VMEM((ROWS, COLS, CH), BF), in_spec...  90.2 us

profile of v4, /device:TPU:1, one launch (start us, length us, event | category | flops | bytes accessed | tf_op | source)
XLA Modules:
  0.0 91.2 jit_solution(18215283523931113627)
XLA Ops:
  0.0 90.2 %layer.1 = bf16[8,256,256]{2,1,0:T(8,128)(2,1)S(1)} custom-call(bf16[8,256,256]{2,1,0:T(8,128)(2,1)} %field.1, s32[8,25]{1,0:T(8,128)} %basis.1, bf16[8,25]{1,0:T(8,128)(2,1)} %quad.1, bf16[4,2,128,128]{3,2,1,0:T(8,128)(2,1)} %mix_w.1, s32[4,128]{1,0:T(4,128)} %bitcast.1, s32[512]{0:T(512)} %modes.1, bf16[2,512,512]{2,1,0:T(8,128)(2,1)} %legendre.1, ...), custom_call_target="tpu_custom_call" | custom-call | tf_op jit(solution)/shard_map/layer/pallas_call | solution.py:610
  90.2 1.0 %copy.13 = bf16[8,256,256]{2,1,0:T(8,128)(2,1)} copy(bf16[8,256,256]{2,1,0:T(8,128)(2,1)S(1)} %layer.1) | data formatting | bytes 2097152
